TPU v7x, 32 devices: a whole 2x2x4 slice. The times are simulated.
32 devices in a mesh: seq: 4 (over y, x), mem: 8 (over z, core).
Axes of the slice: x: 2, y: 2, z: 4, core: 2. Of those that a mesh axis runs over, the one named last changes fastest.
Arguments:
- tokens: bfloat16 [8, 1024, 1024], P('mem', 'seq'), may hold values from -6 to 6
- cached_keys: bfloat16 [8, 8192, 1024], P(None, 'mem'), may hold values from -6 to 6
- cached_values: bfloat16 [8, 8192, 1024], P(None, 'mem'), may hold values from -6 to 6
- knn_index: int32 [8, 1024, 128], P('mem', 'seq'), may hold values from 0 to 8191, as said below
- has_memory: int32 [8], P('mem'), may hold values from 0 to 1, as said below
- w_query: bfloat16 [1024, 1024], P(('seq', 'mem')), may hold values from -0.1875 to 0.1875
- w_key: bfloat16 [1024, 1024], P(('seq', 'mem')), may hold values from -0.1875 to 0.1875
- w_value: bfloat16 [1024, 1024], P(('seq', 'mem')), may hold values from -0.1875 to 0.1875
- w_out: bfloat16 [1024, 1024], P(('seq', 'mem')), may hold values from -1.5 to 1.5
- gain_attn: bfloat16 [1024], P(('seq', 'mem')), may hold values from 0.099609375 to 1.8984375
- w_gate: bfloat16 [1024, 2816], P(('seq', 'mem')), may hold values from -0.1875 to 0.1875
- w_up: bfloat16 [1024, 2816], P(('seq', 'mem')), may hold values from -0.1875 to 0.1875
- w_down: bfloat16 [2816, 1024], P(('seq', 'mem')), may hold values from -0.109375 to 0.109375
- gain_ffn: bfloat16 [1024], P(('seq', 'mem')), may hold values from 0.099609375 to 1.8984375
- cotangent: bfloat16 [8, 1024, 1024], P('mem', 'seq'), may hold values from -6 to 6
Outputs:
- mixed: float32 [8, 1024, 1024], P('mem', 'seq')
- grad_tokens: float32 [8, 1024, 1024], P('mem', 'seq')
- grad_w_query: float32 [1024, 1024], P(('seq', 'mem'))
- grad_w_key: float32 [1024, 1024], P(('seq', 'mem'))
- grad_w_value: float32 [1024, 1024], P(('seq', 'mem'))
- grad_w_out: float32 [1024, 1024], P(('seq', 'mem'))
- grad_gain_attn: float32 [1024], P(('seq', 'mem'))
- grad_w_gate: float32 [1024, 2816], P(('seq', 'mem'))
- grad_w_up: float32 [1024, 2816], P(('seq', 'mem'))
- grad_w_down: float32 [2816, 1024], P(('seq', 'mem'))
- grad_gain_ffn: float32 [1024], P(('seq', 'mem'))
Inputs may be any that keep to these rules, and one draw needn't show every extreme that they name: `knn_index`: each row holds 128 different indices of the 8192 cached keys of its segment. `has_memory`: exactly half of the 8 segments have 1.
All inputs are finite; a program needn't handle non-finite values.
Results may differ from a plain program's by a relative error of at most 0.03.
Values may be sent and summed in bfloat16 or wider, within the bound.
A program may use at most 640 MiB of HBM per device.

v0:
```python
import jax
import jax.numpy as jnp
from jax import lax
from jax.sharding import PartitionSpec as P

HEADS = 8


FLOOR_SCORE = -1e30
EPSILON = 1e-05


def rms_norm(values, gain):
    return values * lax.rsqrt(jnp.mean(values * values, axis=-1, keepdims=True) + EPSILON) * gain


def swiglu(gate_in, up_in):
    return jax.nn.silu(gate_in) * up_in


def angles_for(positions, head_width):
    exponent = jnp.arange(head_width // 2, dtype=jnp.float32) * (2.0 / head_width)
    frequency = jnp.power(10000.0, -exponent)
    turned = positions.astype(jnp.float32)[:, None] * frequency[None, :]
    return (jnp.cos(turned), jnp.sin(turned))


def rotate(values, cosine, sine, head_count):
    leading = values.shape[:-1]
    split = values.reshape(leading + (head_count, values.shape[-1] // head_count))
    middle = split.shape[-1] // 2
    first_half = split[..., :middle]
    second_half = split[..., middle:]
    cos_rows = cosine[:, None, :]
    sin_rows = sine[:, None, :]
    turned = jnp.concatenate(
        [
            first_half * cos_rows - second_half * sin_rows,
            second_half * cos_rows + first_half * sin_rows,
        ],
        axis=-1,
    )
    return turned.reshape(values.shape)


def head_slice(matrix, which, head_width):
    return lax.dynamic_slice_in_dim(matrix, which * head_width, head_width, 1)


def masked_scores(query_part, key_part, allowed, score_scale):
    raw_scores = (
        jnp.einsum("qd,kd->qk", query_part, key_part, preferred_element_type=jnp.float32)
        * score_scale
    )
    return jnp.where(allowed, raw_scores, FLOOR_SCORE)


def merge_heads(stacked):
    return jnp.moveaxis(stacked, 0, 1).reshape(stacked.shape[1], -1)


def column_product(left, right):
    return jnp.einsum("tr,te->re", left, right, preferred_element_type=jnp.float32)


def per_device(
    tokens,
    cached_keys,
    cached_values,
    knn_index,
    has_memory,
    w_query,
    w_key,
    w_value,
    w_out,
    gain_attn,
    w_gate,
    w_up,
    w_down,
    gain_ffn,
    cotangent,
):
    (
        query_weight,
        key_weight,
        value_weight,
        out_weight,
        gain_first,
        gate_weight,
        up_weight,
        down_weight,
        gain_second,
    ) = (
        lax.all_gather(w_query, ("seq", "mem"), axis=0, tiled=True),
        lax.all_gather(w_key, ("seq", "mem"), axis=0, tiled=True),
        lax.all_gather(w_value, ("seq", "mem"), axis=0, tiled=True),
        lax.all_gather(w_out, ("seq", "mem"), axis=0, tiled=True),
        lax.all_gather(gain_attn, ("seq", "mem"), axis=0, tiled=True),
        lax.all_gather(w_gate, ("seq", "mem"), axis=0, tiled=True),
        lax.all_gather(w_up, ("seq", "mem"), axis=0, tiled=True),
        lax.all_gather(w_down, ("seq", "mem"), axis=0, tiled=True),
        lax.all_gather(gain_ffn, ("seq", "mem"), axis=0, tiled=True),
    )
    inputs = tokens[0].astype(jnp.float32)
    row_count = inputs.shape[0]
    feature_width = inputs.shape[1]
    hidden_width = gate_weight.shape[1]
    head_count = HEADS
    head_width = feature_width // head_count
    score_scale = head_width ** (-0.5)
    head_ids = jnp.arange(head_count)
    positions = lax.axis_index("seq") * row_count + jnp.arange(row_count)
    cosine, sine = angles_for(positions, head_width)
    segment_length = row_count * lax.axis_size("seq")
    causal = jnp.arange(segment_length)[None, :] <= positions[:, None]
    mem_dev = cached_keys.shape[1]
    memory_total = mem_dev * lax.axis_size("mem")
    live_index = jnp.where(has_memory[0] > 0, knn_index[0], memory_total)
    row_ids = jnp.arange(row_count)[:, None]
    normed_one, norm_one_back = jax.vjp(rms_norm, inputs, gain_first.astype(jnp.float32))
    norm_one = normed_one.astype(jnp.bfloat16)
    queries = rotate(
        jnp.dot(norm_one, query_weight, preferred_element_type=jnp.float32),
        cosine,
        sine,
        head_count,
    ).astype(jnp.bfloat16)
    keys = rotate(
        jnp.dot(norm_one, key_weight, preferred_element_type=jnp.float32), cosine, sine, head_count
    ).astype(jnp.bfloat16)
    values = jnp.dot(norm_one, value_weight, preferred_element_type=jnp.float32).astype(
        jnp.bfloat16
    )
    segment_keys, segment_values = (
        lax.all_gather(keys, "seq", axis=0, tiled=True),
        lax.all_gather(values, "seq", axis=0, tiled=True),
    )

    def local_stats(which):
        query_part = head_slice(queries, which, head_width)
        local_scores = masked_scores(
            query_part, head_slice(segment_keys, which, head_width), causal, score_scale
        )
        row_max = jnp.max(local_scores, 1)
        return (local_scores, row_max, jnp.sum(jnp.exp(local_scores - row_max[:, None]), 1))

    kept_scores, local_max, local_sum = lax.map(local_stats, head_ids)
    all_queries, all_index = (
        lax.all_gather(queries[None], "mem", axis=0, tiled=True),
        lax.all_gather(live_index[None], "mem", axis=0, tiled=True),
    )
    base_index = lax.axis_index("mem") * mem_dev

    def owner_scores(items):
        query_piece, index_piece, key_piece = items
        offsets = index_piece - base_index
        offsets = jnp.where((offsets >= 0) & (offsets < mem_dev), offsets, mem_dev)
        permitted = (
            jnp.zeros((row_count, mem_dev), jnp.bool_).at[row_ids, offsets].set(True, mode="drop")
        )
        raw_scores = (
            jnp.einsum(
                "qhd,khd->hqk",
                query_piece.reshape(row_count, head_count, head_width),
                key_piece.reshape(mem_dev, head_count, head_width),
                preferred_element_type=jnp.float32,
            )
            * score_scale
        )
        piece_scores = jnp.where(permitted[None], raw_scores, FLOOR_SCORE)
        piece_max = jnp.max(piece_scores, 2)
        piece_sum = jnp.sum(
            jnp.where(permitted[None], jnp.exp(piece_scores - piece_max[..., None]), 0.0), 2
        )
        return (piece_scores, piece_max, piece_sum)

    owner_kept, owner_max, owner_sum = lax.map(owner_scores, (all_queries, all_index, cached_keys))
    peer_max, peer_sum = (
        lax.all_to_all(
            owner_max.astype(jnp.bfloat16), "mem", split_axis=0, concat_axis=0, tiled=True
        ).astype(owner_max.dtype),
        lax.all_to_all(
            owner_sum.astype(jnp.bfloat16), "mem", split_axis=0, concat_axis=0, tiled=True
        ).astype(owner_sum.dtype),
    )
    row_max = jnp.maximum(local_max, jnp.max(peer_max, 0))
    row_sum = local_sum * jnp.exp(local_max - row_max) + jnp.sum(
        peer_sum * jnp.exp(peer_max - row_max[None]), 0
    )
    log_total = row_max + jnp.log(row_sum)
    all_totals = lax.all_gather(log_total[None], "mem", axis=0, tiled=True)

    def owner_outputs(items):
        piece_scores, piece_total, value_piece = items
        piece_weights = jnp.exp(piece_scores - piece_total[..., None]).astype(jnp.bfloat16)
        summed = jnp.einsum(
            "hqk,khd->qhd",
            piece_weights,
            value_piece.reshape(mem_dev, head_count, head_width),
            preferred_element_type=jnp.float32,
        )
        return summed.reshape(row_count, feature_width)

    owner_out = lax.map(owner_outputs, (owner_kept, all_totals, cached_values))
    peer_out = lax.all_to_all(
        owner_out.astype(jnp.bfloat16), "mem", split_axis=0, concat_axis=0, tiled=True
    ).astype(owner_out.dtype)

    def local_outputs(items):
        local_scores, log_row, which = items
        local_weights = jnp.exp(local_scores - log_row[:, None]).astype(jnp.bfloat16)
        return jnp.dot(
            local_weights,
            head_slice(segment_values, which, head_width),
            preferred_element_type=jnp.float32,
        )

    memory_part = jnp.moveaxis(
        jnp.sum(peer_out, 0).reshape(row_count, head_count, head_width), 1, 0
    )
    head_outputs = lax.map(local_outputs, (kept_scores, log_total, head_ids)) + memory_part
    attention = merge_heads(head_outputs)
    attention_low = attention.astype(jnp.bfloat16)
    mid = inputs + jnp.dot(attention_low, out_weight, preferred_element_type=jnp.float32)
    normed_two, norm_two_back = jax.vjp(rms_norm, mid, gain_second.astype(jnp.float32))
    norm_two = normed_two.astype(jnp.bfloat16)
    gate = jnp.dot(norm_two, gate_weight, preferred_element_type=jnp.float32)
    upward = jnp.dot(norm_two, up_weight, preferred_element_type=jnp.float32)
    gated, gated_back = jax.vjp(swiglu, gate, upward)
    hidden = gated.astype(jnp.bfloat16)
    mixed = mid + jnp.dot(hidden, down_weight, preferred_element_type=jnp.float32)
    grad_out = cotangent[0]
    grad_hidden = jnp.einsum("td,fd->tf", grad_out, down_weight, preferred_element_type=jnp.float32)
    grad_gate_full, grad_up_full = gated_back(grad_hidden)
    grad_gate = grad_gate_full.astype(jnp.bfloat16)
    grad_upward = grad_up_full.astype(jnp.bfloat16)
    grad_norm_two = jnp.einsum(
        "tf,df->td", grad_gate, gate_weight, preferred_element_type=jnp.float32
    )
    grad_norm_two = grad_norm_two + jnp.einsum(
        "tf,df->td", grad_upward, up_weight, preferred_element_type=jnp.float32
    )
    grad_mid_norm, grad_gain_second = norm_two_back(grad_norm_two)
    grad_mid = grad_out.astype(jnp.float32) + grad_mid_norm
    grad_mid_low = grad_mid.astype(jnp.bfloat16)
    grad_attention = jnp.einsum(
        "te,de->td", grad_mid_low, out_weight, preferred_element_type=jnp.float32
    ).astype(jnp.bfloat16)
    grad_dots = jnp.sum(
        (grad_attention.astype(jnp.float32) * attention).reshape(row_count, head_count, head_width),
        axis=2,
    ).T

    def local_backward(items):
        local_scores, log_row, dots_row, which = items
        query_part = head_slice(queries, which, head_width)
        grad_part = head_slice(grad_attention, which, head_width)
        key_local = head_slice(segment_keys, which, head_width)
        value_local = head_slice(segment_values, which, head_width)
        local_weights = jnp.exp(local_scores - log_row[:, None])
        local_dweights = jnp.einsum(
            "qd,kd->qk", grad_part, value_local, preferred_element_type=jnp.float32
        )
        local_dscore = (local_weights * (local_dweights - dots_row[:, None]) * score_scale).astype(
            jnp.bfloat16
        )
        grad_query = jnp.einsum(
            "qk,kd->qd", local_dscore, key_local, preferred_element_type=jnp.float32
        )
        grad_key = jnp.einsum(
            "qk,qd->kd", local_dscore, query_part, preferred_element_type=jnp.float32
        )
        grad_value = jnp.einsum(
            "qk,qd->kd",
            local_weights.astype(jnp.bfloat16),
            grad_part,
            preferred_element_type=jnp.float32,
        )
        return (grad_query, grad_key, grad_value)

    head_dq, head_dk, head_dv = lax.map(
        local_backward, (kept_scores, log_total, grad_dots, head_ids)
    )
    all_grads = lax.all_gather(grad_attention[None], "mem", axis=0, tiled=True)
    all_dots = lax.all_gather(grad_dots[None], "mem", axis=0, tiled=True)

    def owner_backward(items):
        piece_scores, piece_total, piece_dots, grad_piece, value_piece, key_piece = items
        piece_weights = jnp.exp(piece_scores - piece_total[..., None])
        piece_dweights = jnp.einsum(
            "qhd,khd->hqk",
            grad_piece.reshape(row_count, head_count, head_width),
            value_piece.reshape(mem_dev, head_count, head_width),
            preferred_element_type=jnp.float32,
        )
        piece_dscore = (
            piece_weights * (piece_dweights - piece_dots[..., None]) * score_scale
        ).astype(jnp.bfloat16)
        summed = jnp.einsum(
            "hqk,khd->qhd",
            piece_dscore,
            key_piece.reshape(mem_dev, head_count, head_width),
            preferred_element_type=jnp.float32,
        )
        return summed.reshape(row_count, feature_width)

    owner_grads = lax.map(
        owner_backward, (owner_kept, all_totals, all_dots, all_grads, cached_values, cached_keys)
    )
    peer_grads = lax.all_to_all(
        owner_grads.astype(jnp.bfloat16), "mem", split_axis=0, concat_axis=0, tiled=True
    ).astype(owner_grads.dtype)
    grad_queries = merge_heads(head_dq) + jnp.sum(peer_grads, 0)
    grad_keys_mine, grad_values_mine = (
        lax.psum_scatter(
            merge_heads(head_dk).astype(jnp.bfloat16), "seq", scatter_dimension=0, tiled=True
        ).astype(jnp.float32),
        lax.psum_scatter(
            merge_heads(head_dv).astype(jnp.bfloat16), "seq", scatter_dimension=0, tiled=True
        ).astype(jnp.float32),
    )
    grad_query_in = rotate(grad_queries, cosine, -sine, head_count).astype(jnp.bfloat16)
    grad_key_in = rotate(grad_keys_mine, cosine, -sine, head_count).astype(jnp.bfloat16)
    grad_value_in = grad_values_mine.astype(jnp.bfloat16)
    grad_norm_one = jnp.einsum(
        "te,de->td", grad_query_in, query_weight, preferred_element_type=jnp.float32
    )
    grad_norm_one = grad_norm_one + jnp.einsum(
        "te,de->td", grad_key_in, key_weight, preferred_element_type=jnp.float32
    )
    grad_norm_one = grad_norm_one + jnp.einsum(
        "te,de->td", grad_value_in, value_weight, preferred_element_type=jnp.float32
    )
    grad_in_norm, grad_gain_first = norm_one_back(grad_norm_one)
    grad_inputs = grad_mid + grad_in_norm
    pieces = [
        column_product(norm_one, grad_query_in),
        column_product(norm_one, grad_key_in),
        column_product(norm_one, grad_value_in),
        column_product(attention_low, grad_mid_low),
        column_product(norm_two, grad_gate),
        column_product(norm_two, grad_upward),
        grad_gain_first[:, None],
        grad_gain_second[:, None],
    ]
    summed_rows = lax.psum_scatter(
        jnp.concatenate(pieces, axis=1), ("seq", "mem"), scatter_dimension=0, tiled=True
    )
    summed_down = lax.psum_scatter(
        column_product(hidden, grad_out), ("seq", "mem"), scatter_dimension=0, tiled=True
    )
    grad_query_weight = summed_rows[:, 0:feature_width]
    grad_key_weight = summed_rows[:, feature_width : 2 * feature_width]
    grad_value_weight = summed_rows[:, 2 * feature_width : 3 * feature_width]
    grad_out_weight = summed_rows[:, 3 * feature_width : 4 * feature_width]
    grad_gate_weight = summed_rows[:, 4 * feature_width : 4 * feature_width + hidden_width]
    grad_up_weight = summed_rows[
        :, 4 * feature_width + hidden_width : 4 * feature_width + 2 * hidden_width
    ]
    gain_one_rows = summed_rows[:, 4 * feature_width + 2 * hidden_width]
    gain_two_rows = summed_rows[:, 4 * feature_width + 2 * hidden_width + 1]
    return (
        mixed[None],
        grad_inputs[None],
        grad_query_weight,
        grad_key_weight,
        grad_value_weight,
        grad_out_weight,
        gain_one_rows,
        grad_gate_weight,
        grad_up_weight,
        summed_down,
        gain_two_rows,
    )


def solution(mesh):
    return jax.shard_map(
        per_device,
        mesh=mesh,
        in_specs=(
            P("mem", "seq", None),
            P(None, "mem", None),
            P(None, "mem", None),
            P("mem", "seq", None),
            P("mem"),
            P(("seq", "mem"), None),
            P(("seq", "mem"), None),
            P(("seq", "mem"), None),
            P(("seq", "mem"), None),
            P(("seq", "mem")),
            P(("seq", "mem"), None),
            P(("seq", "mem"), None),
            P(("seq", "mem"), None),
            P(("seq", "mem")),
            P("mem", "seq", None),
        ),
        out_specs=(
            P("mem", "seq", None),
            P("mem", "seq", None),
            P(("seq", "mem"), None),
            P(("seq", "mem"), None),
            P(("seq", "mem"), None),
            P(("seq", "mem"), None),
            P(("seq", "mem")),
            P(("seq", "mem"), None),
            P(("seq", "mem"), None),
            P(("seq", "mem"), None),
            P(("seq", "mem")),
        ),
        check_vma=False,
    )
```

profile of v0, /device:TPU:0, one launch (start us, length us, event | category | flops | bytes accessed | tf_op | source)
XLA Modules:
  0.0 2690.8 jit_solution(17476410549669014485)
XLA Ops:
  12.6 42.9 %all-reduce.2 = (bf16[1024]{0:T(1024)(128)(2,1)S(1)}, bf16[1024]{0:T(1024)(128)(2,1)S(1)}) all-reduce(bf16[1024]{0:T(1024)(128)(2,1)S(1)} %dynamic-update-slice, bf16[1024]{0:T(1024)(128)(2,1)S(1)} %dynamic-update-slice.1), channel_id=1, replica_groups=mesh['seq'=4,'mem'=8] {'seq','mem'}, use_global_device_ids=true, to_apply=%add | all-reduce | flops 2048 | bytes 8192
  57.7 12.7 all-gather.16.cloned.1.call-done
  75.3 53.4 %all-gather.18.cloned.1.call-done = bf16[1024,1024]{1,0:T(8,128)(2,1)} async-done(((bf16[32,1024]{1,0:T(8,128)(2,1)}), bf16[1024,1024]{1,0:T(8,128)(2,1)}) %all-gather.18.cloned.1.call-update) | async-done | bytes 2097168 | tf_op jit(solution)/shard_map/all_gather | solution.py:95
  133.7 53.4 %all-gather.26.cloned.1.call-done = bf16[1024,1024]{1,0:T(8,128)(2,1)} async-done(((bf16[32,1024]{1,0:T(8,128)(2,1)}), bf16[1024,1024]{1,0:T(8,128)(2,1)}) %all-gather.26.cloned.1.call-update) | async-done | bytes 2097168 | tf_op jit(solution)/shard_map/all_gather | solution.py:96
  193.1 21.7 copy.133
  214.8 21.8 copy.135
  237.6 21.3 all-gather.24.cloned.1.call-done
  258.9 1215.0 %while.79 = (s32[]{:T(128)}, f32[8,8,256,1024]{3,2,1,0:T(8,128)}, bf16[8,8,256]{2,1,0:T(8,128)(2,1)}, bf16[8,8,256]{2,1,0:T(8,128)(2,1)}, s32[8,256,128]{2,1,0:T...) while((s32[]{:T(128)}, f32[8,8,256,1024]{3,2,1,0:T(8,128)}, ...), condition=%wide.region_9.10_spmd.clone, body=%wide.region_5.9_spmd.clone.sunk | while | flops 558592000 | bytes 45495968 | solution.py:177
  260.1 136.7 %scatter_custom_fusion.6 = pred[262144]{0:T(1024)(128)(4,1)S(1)} fusion(s32[32768]{0:T(1024)S(1)} %select_bitcast_fusion.2, pred[32768]{0:T(1024)(128)(4,1)S(1)} %broadcast.348, pred[]{:T(512)} %constant.84.clone.2..sunk), kind=kCustom, calls=%fused_computation.73.clone.1 | custom fusion | bytes 262145 | tf_op jit(solution)/shard_map/while
  412.0 136.7 %scatter_custom_fusion.6 = pred[262144]{0:T(1024)(128)(4,1)S(1)} fusion(s32[32768]{0:T(1024)S(1)} %select_bitcast_fusion.2, pred[32768]{0:T(1024)(128)(4,1)S(1)} %broadcast.348, pred[]{:T(512)} %constant.84.clone.2..sunk), kind=kCustom, calls=%fused_computation.73.clone.1 | custom fusion | bytes 262145 | tf_op jit(solution)/shard_map/while
  563.9 136.7 %scatter_custom_fusion.6 = pred[262144]{0:T(1024)(128)(4,1)S(1)} fusion(s32[32768]{0:T(1024)S(1)} %select_bitcast_fusion.2, pred[32768]{0:T(1024)(128)(4,1)S(1)} %broadcast.348, pred[]{:T(512)} %constant.84.clone.2..sunk), kind=kCustom, calls=%fused_computation.73.clone.1 | custom fusion | bytes 262145 | tf_op jit(solution)/shard_map/while
  715.8 136.7 %scatter_custom_fusion.6 = pred[262144]{0:T(1024)(128)(4,1)S(1)} fusion(s32[32768]{0:T(1024)S(1)} %select_bitcast_fusion.2, pred[32768]{0:T(1024)(128)(4,1)S(1)} %broadcast.348, pred[]{:T(512)} %constant.84.clone.2..sunk), kind=kCustom, calls=%fused_computation.73.clone.1 | custom fusion | bytes 262145 | tf_op jit(solution)/shard_map/while
  867.6 136.7 %scatter_custom_fusion.6 = pred[262144]{0:T(1024)(128)(4,1)S(1)} fusion(s32[32768]{0:T(1024)S(1)} %select_bitcast_fusion.2, pred[32768]{0:T(1024)(128)(4,1)S(1)} %broadcast.348, pred[]{:T(512)} %constant.84.clone.2..sunk), kind=kCustom, calls=%fused_computation.73.clone.1 | custom fusion | bytes 262145 | tf_op jit(solution)/shard_map/while
  1019.5 136.7 %scatter_custom_fusion.6 = pred[262144]{0:T(1024)(128)(4,1)S(1)} fusion(s32[32768]{0:T(1024)S(1)} %select_bitcast_fusion.2, pred[32768]{0:T(1024)(128)(4,1)S(1)} %broadcast.348, pred[]{:T(512)} %constant.84.clone.2..sunk), kind=kCustom, calls=%fused_computation.73.clone.1 | custom fusion | bytes 262145 | tf_op jit(solution)/shard_map/while
  1171.4 136.7 %scatter_custom_fusion.6 = pred[262144]{0:T(1024)(128)(4,1)S(1)} fusion(s32[32768]{0:T(1024)S(1)} %select_bitcast_fusion.2, pred[32768]{0:T(1024)(128)(4,1)S(1)} %broadcast.348, pred[]{:T(512)} %constant.84.clone.2..sunk), kind=kCustom, calls=%fused_computation.73.clone.1 | custom fusion | bytes 262145 | tf_op jit(solution)/shard_map/while
  1323.2 136.7 %scatter_custom_fusion.6 = pred[262144]{0:T(1024)(128)(4,1)S(1)} fusion(s32[32768]{0:T(1024)S(1)} %select_bitcast_fusion.2, pred[32768]{0:T(1024)(128)(4,1)S(1)} %broadcast.348, pred[]{:T(512)} %constant.84.clone.2..sunk), kind=kCustom, calls=%fused_computation.73.clone.1 | custom fusion | bytes 262145 | tf_op jit(solution)/shard_map/while
  1477.3 32.8 %while.78 = (s32[]{:T(128)}, f32[8,256,1024]{2,1,0:T(8,128)}, f32[8,256]{1,0:T(8,128)S(1)}, f32[8,256]{1,0:T(8,128)S(1)}, s32[8]{0:T(128)S(1)}, /*index=5*/bf16[...) while((s32[]{:T(128)}, f32[8,256,1024]{2,1,0:T(8,128)}, ...), condition=%wide.region_4.5_spmd.clone, body=%wide.region_1.4_spmd.clone.sunk | while | flops 68681224 | bytes 4531907 | solution.py:147
  1520.9 14.0 all-gather
  1537.0 61.8 %while.75 = (s32[]{:T(128)}, bf16[8,256,1024]{1,2,0:T(8,128)(2,1)}, bf16[8,1024,1024]{1,2,0:T(8,128)(2,1)}, f32[8,8,256,1024]{3,2,1,0:T(8,128)}, f32[8,8,256]{2,1,0:T(8,128)S(1)}, /*index=5*/s32[]{:T(128)}) while((s32[]{:T(128)}, bf16[8,256,1024]{1,2,0:T(8,128)(2,1)}, bf16[8,1024,1024]{1,2,0:T(8,128)(2,1)}, f32[8,8,256,1024]{3,2,1,0:T(8,128)}, ...), condition=%wide.region_15.16_spmd, body=%wide.region_14.15_spmd.sunk | while | flops 541065216 | bytes 16278605 | solution.py:204
  1604.0 23.5 while.74
  1627.6 69.8 %all-to-all-done.2 = bf16[8,256,1024]{1,2,0:T(8,128)(2,1)} async-done(((bf16[8,256,1024]{1,2,0:T(8,128)(2,1)}), bf16[8,256,1024]{1,2,0:T(8,128)(2,1)}, u32[]{:S(2)}, u32[]{:S(2)}) %all-to-all-start.2) | async-done | bytes 4194336 | tf_op jit(solution)/shard_map/all_to_all | solution.py:205
  1715.8 8.3 multiply_convert_fusion
  1737.0 14.4 all-gather.2
  1751.5 67.5 %while.76 = (s32[]{:T(128)}, f32[8,256,128]{1,2,0:T(8,128)S(1)}, bf16[8,1024,128]{1,2,0:T(8,128)(2,1)}, bf16[8,1024,128]{1,2,0:T(8,128)(2,1)}, f32[8,256,1024]{2...) while((s32[]{:T(128)}, f32[8,256,128]{1,2,0:T(8,128)S(1)}, ...), condition=%wide.region_21.22_spmd, body=%wide.region_20.21_spmd.sunk | while | flops 270270464 | bytes 5581535 | solution.py:281
  1821.3 117.1 %while.77 = (s32[]{:T(128)}, bf16[8,256,1024]{1,2,0:T(8,128)(2,1)}, bf16[8,1024,1024]{1,2,0:T(8,128)(2,1)}, f32[8,8,256,1024]{3,2,1,0:T(8,128)}, f32[8,8,256]{2,...) while((s32[]{:T(128)}, bf16[8,256,1024]{1,2,0:T(8,128)(2,1)}, ...), condition=%wide.region_23.24_spmd, body=%wide.region_22.23_spmd.sunk | while | flops 1084227584 | bytes 25216104 | solution.py:307
  1827.4 7.9 fusion.197
  1842.3 7.9 fusion.197
  1960.6 22.8 reduce-scatter.7.cloned.1.call-done
  1987.3 49.8 %all-to-all-done.3 = bf16[8,256,1024]{1,2,0:T(8,128)(2,1)} async-done(((bf16[8,256,1024]{1,2,0:T(8,128)(2,1)}), bf16[8,256,1024]{1,2,0:T(8,128)(2,1)}, u32[]{:S(2)}, u32[]{:S(2)}) %all-to-all-start.3) | async-done | bytes 4194336 | tf_op jit(solution)/shard_map/all_to_all | solution.py:310
  2050.4 42.6 %concatenate.23 = f32[1024,9730]{1,0:T(8,128)} concatenate(f32[1024,1024]{1,0:T(8,128)} %fusion.84, f32[1024,1024]{1,0:T(8,128)} %fusion.82, f32[1024,1024]{1,0:T(8,128)} %fusion.91, f32[1024,1024]{1,0:T(8,128)} %fusion.86, f32[1024,2816]{1,0:T(8,128)} %fusion.108, f32[1024,2816]{1,0:T(8,128)} %fusion.109, f32[1024,1]{1,0:T(8,128)S(1)} %copy.152, f32[1024,1]{1,0:T(8,128)S(1)} %copy-done.17), dimensions={1} | concatenate | bytes 79708160 | tf_op jit(solution)/shard_map/concatenate | solution.py:347
  2110.2 413.9 %reduce-scatter.9.cloned.1.call-done = f32[32,9730]{1,0:T(8,128)} async-done(((f32[1024,9730]{1,0:T(8,128)}), f32[32,9730]{1,0:T(8,128)}) %reduce-scatter.9.cloned.1.call-update) | async-done | bytes 1245456 | tf_op jit(solution)/shard_map/reduce_scatter | solution.py:346
  2529.4 154.7 %reduce-scatter.11.cloned.1.call-done = f32[88,1024]{1,0:T(8,128)} async-done(((f32[2816,1024]{1,0:T(8,128)}), f32[88,1024]{1,0:T(8,128)}) %reduce-scatter.11.cloned.1.call-update) | async-done | bytes 360464 | tf_op jit(solution)/shard_map/reduce_scatter | solution.py:349
  (525 shorter events, 531.2 us)
Async XLA Ops:
  7.2 66.0 %copy-start = (bf16[1,256,1024]{2,1,0:T(8,128)(2,1)S(1)}, bf16[1,256,1024]{2,1,0:T(8,128)(2,1)}, u32[]{:S(2)}) copy-start(bf16[1,256,1024]{2,1,0:T(8,128)(2,1)} %param.27) | copy-start | bytes 1572868
  7.2 63.2 %all-gather.16.cloned.1.call-start = ((), (), s32[]{:S(2)}) async-start(), calls=%async_computation.8 | async-start | bytes 2162688 | tf_op jit(solution)/shard_map/all_gather | solution.py:94
  7.9 120.8 %all-gather.18.cloned.1.call-start = ((), (), s32[]{:S(2)}) async-start(), calls=%async_computation.9 | async-start | bytes 2162688 | tf_op jit(solution)/shard_map/all_gather | solution.py:95
  8.7 178.4 %all-gather.26.cloned.1.call-start = ((), (), s32[]{:S(2)}) async-start(), calls=%async_computation.13 | async-start | bytes 2162688 | tf_op jit(solution)/shard_map/all_gather | solution.py:96
  9.4 228.2 %all-gather.22.cloned.1.call-start = ((), (), s32[]{:S(2)}) async-start(), calls=%async_computation.11 | async-start | bytes 1179648 | tf_op jit(solution)/shard_map/all_gather | solution.py:150
  10.8 248.1 %all-gather.24.cloned.1.call-start = ((), (), s32[]{:S(2)}) async-start(), calls=%async_computation.12 | async-start | bytes 4718592 | tf_op jit(solution)/shard_map/all_gather | solution.py:149
  55.5 131.6 %copy-start.29 = (f32[1024]{0:T(1024)}, f32[1024]{0:T(1024)S(1)}, u32[]{:S(2)}) copy-start(f32[1024]{0:T(1024)S(1)} %convert_element_type.175) | copy-start | bytes 12292
  56.7 130.3 %copy-start.31 = (f32[256]{0:T(256)}, f32[256]{0:T(256)S(1)}, u32[]{:S(2)}) copy-start(f32[256]{0:T(256)S(1)} %fusion.95) | copy-start | bytes 3076
  57.7 74.7 %copy-start.26 = (f32[256,64]{0,1:T(8,128)}, f32[256,64]{0,1:T(8,128)S(1)}, u32[]{:S(2)}) copy-start(f32[256,64]{0,1:T(8,128)S(1)} %get-tuple-element.648) | copy-start | bytes 196612
  75.3 1402.0 %all-gather.20.cloned.1.call-start = ((), (), s32[]{:S(2)}) async-start(), calls=%async_computation.10 | async-start | bytes 2621440 | tf_op jit(solution)/shard_map/all_gather | solution.py:135
  133.6 1470.3 %all-gather.28.cloned.1.call-start = ((), (), s32[]{:S(2)}) async-start(), calls=%async_computation.14 | async-start | bytes 2621440 | tf_op jit(solution)/shard_map/all_gather | solution.py:136
  190.2 1510.6 %all-gather.30.cloned.1.call-start = ((), (), s32[]{:S(2)}) async-start(), calls=%async_computation.15 | async-start | bytes 2162688 | tf_op jit(solution)/shard_map/all_gather | solution.py:97
  191.0 1512.8 %all-gather.32.cloned.1.call-start = ((), (), s32[]{:S(2)}) async-start(), calls=%async_computation.16 | async-start | bytes 5947392 | tf_op jit(solution)/shard_map/all_gather | solution.py:99
  191.7 1518.2 %all-gather.34.cloned.1.call-start = ((), (), s32[]{:S(2)}) async-start(), calls=%async_computation.17 | async-start | bytes 5947392 | tf_op jit(solution)/shard_map/all_gather | solution.py:100
  192.3 1523.6 %all-gather.36.cloned.1.call-start = ((), (), s32[]{:S(2)}) async-start(), calls=%async_computation.18 | async-start | bytes 5947392 | tf_op jit(solution)/shard_map/all_gather | solution.py:101
  214.8 44.1 %copy-start.33 = (s32[2]{0:T(128)S(1)}, s32[2]{0:T(128)}, u32[]{:S(2)}) copy-start(s32[2]{0:T(128)} %constant.295) | copy-start | bytes 28
  214.8 44.1 %copy-start.34 = (s32[2]{0:T(128)S(1)}, s32[2]{0:T(128)}, u32[]{:S(2)}) copy-start(s32[2]{0:T(128)} %constant.296) | copy-start | bytes 28
  1473.9 36.2 %all-to-all-start = ((bf16[8,8,256]{2,1,0:T(8,128)(2,1)}), bf16[8,8,256]{2,1,0:T(8,128)(2,1)S(1)}, u32[]{:S(2)}, u32[]{:S(2)}) async-start(bf16[8,8,256]{2,1,0:T(8,128)(2,1)} %get-tuple-element.271), calls=%async_computation | async-start | bytes 65536 | tf_op jit(solution)/shard_map/all_to_all | solution.py:179
  1510.1 10.7 all-to-all-start.1
  1598.8 98.6 %all-to-all-start.2 = ((bf16[8,256,1024]{1,2,0:T(8,128)(2,1)}), bf16[8,256,1024]{1,2,0:T(8,128)(2,1)}, u32[]{:S(2)}, u32[]{:S(2)}) async-start(bf16[8,256,1024]{1,2,0:T(8,128)(2,1)} %get-tuple-element.276), calls=%async_computation.2 | async-start | bytes 8388608 | tf_op jit(solution)/shard_map/all_to_all | solution.py:205
  1603.4 215.6 %all-gather.38.cloned.1.call-start = ((), (), s32[]{:S(2)}) async-start(), calls=%async_computation.23 | async-start | bytes 4718592 | tf_op jit(solution)/shard_map/all_gather | solution.py:284
  1627.6 73.2 %copy-start.1 = (bf16[1,256,1024]{2,1,0:T(8,128)(2,1)S(1)}, bf16[1,256,1024]{2,1,0:T(8,128)(2,1)}, u32[]{:S(2)}) copy-start(bf16[1,256,1024]{2,1,0:T(8,128)(2,1)} %param.27) | copy-start | bytes 1572868
  1700.7 33.2 %copy-start.2 = (f32[256,1024]{1,0:T(8,128)}, f32[256,1024]{1,0:T(8,128)S(1)}, u32[]{:S(2)}) copy-start(f32[256,1024]{1,0:T(8,128)S(1)} %copy.162) | copy-start | bytes 3145732
  1735.2 224.3 %reduce-scatter.5.cloned.1.call-start = ((), (), s32[]{:S(2)}) async-start(), calls=%async_computation.19 | async-start | bytes 2621440 | tf_op jit(solution)/shard_map/reduce_scatter | solution.py:315
  1938.4 98.7 %all-to-all-start.3 = ((bf16[8,256,1024]{1,2,0:T(8,128)(2,1)}), bf16[8,256,1024]{1,2,0:T(8,128)(2,1)}, u32[]{:S(2)}, u32[]{:S(2)}) async-start(bf16[8,256,1024]{1,2,0:T(8,128)(2,1)} %get-tuple-element.278), calls=%async_computation.3 | async-start | bytes 8388608 | tf_op jit(solution)/shard_map/all_to_all | solution.py:310
  1943.1 40.3 %reduce-scatter.7.cloned.1.call-start = ((), (), s32[]{:S(2)}) async-start(), calls=%async_computation.20 | async-start | bytes 2621440 | tf_op jit(solution)/shard_map/reduce_scatter | solution.py:318
  1943.7 580.4 %reduce-scatter.9.cloned.1.call-start = ((), (), s32[]{:S(2)}) async-start(), calls=%async_computation.21 | async-start | bytes 41631744 | tf_op jit(solution)/shard_map/reduce_scatter | solution.py:346
  1953.5 29.9 %copy-start.30 = (f32[1024]{0:T(1024)S(1)}, f32[1024]{0:T(1024)}, u32[]{:S(2)}) copy-start(f32[1024]{0:T(1024)} %copy-done.29) | copy-start | bytes 12292
  1953.5 29.9 %copy-start.32 = (f32[256]{0:T(256)S(1)}, f32[256]{0:T(256)}, u32[]{:S(2)}) copy-start(f32[256]{0:T(256)} %copy-done.31) | copy-start | bytes 3076
  1987.3 52.9 %copy-start.27 = (f32[256,64]{0,1:T(8,128)S(1)}, f32[256,64]{0,1:T(8,128)}, u32[]{:S(2)}) copy-start(f32[256,64]{0,1:T(8,128)} %copy-done.26) | copy-start | bytes 196612
  1987.3 52.9 %copy-start.28 = (f32[256,64]{0,1:T(8,128)S(1)}, f32[256,64]{0,1:T(8,128)}, u32[]{:S(2)}) copy-start(f32[256,64]{0,1:T(8,128)} %get-tuple-element.646) | copy-start | bytes 196612
  2093.1 591.0 %reduce-scatter.11.cloned.1.call-start = ((), (), s32[]{:S(2)}) async-start(), calls=%async_computation.22 | async-start | bytes 11894784 | tf_op jit(solution)/shard_map/reduce_scatter | solution.py:349
  (26 other events, 133.3 us)
Sparse Core Ops, SparseCore 0:
  11.0 59.3 all-gather.15
  73.3 55.3 all-gather.17
  131.7 55.3 all-gather.25
  189.1 20.9 all-gather.21
  212.1 46.7 all-gather.23
  261.2 34.0 all-gather.19
  297.1 35.3 all-gather.27
  335.4 56.4 all-gather.29
  394.8 66.0 all-gather.31
  463.6 66.2 all-gather.33
  532.8 66.2 all-gather.35
  1735.3 46.1 all-gather.37
  1819.1 34.1 reduce-scatter.4
  1946.9 36.5 reduce-scatter.6
  2093.2 430.7 reduce-scatter.8
  2526.9 157.1 reduce-scatter.10
where the time goes:
time: 2700 us; the launch traced here: 2690 us
  local copies, waits for them, and re-layouts  1330 us (49%)
  waiting for transfers between devices  863 us (32%)
  matrix products  310 us (11%)
  blocking collectives  71.2 us (3%)
  other arithmetic  62.1 us (2%)
    while x16, local copies, waits for them, and re-layouts  1090 us
    reduce_scatter x1, waiting for transfers between devices, per_device(): lax.psum_scatter(jnp.concatenate(pieces, axis=1), ('seq', 'mem'), scatter...  414 us
    reduce_scatter x1, waiting for transfers between devices, per_device(): lax.psum_scatter(column_product(hidden, grad_out), ('seq', 'mem'), scatte...  155 us
    dynamic_slice x56, local copies, waits for them, and re-layouts, per_device(): lax.map(owner_scores, (all_queries, all_index, cached_keys))  87.4 us
    all_to_all x1, waiting for transfers between devices, per_device(): lax.all_to_all(owner_out.astype(jnp.bfloat16), 'mem', split_axis=0, conca...  69.8 us
    dot_general x8, matrix products, owner_backward(): jnp.einsum('hqk,khd->qhd', piece_dscore, key_piece.reshape(mem_dev, head_...  61.4 us
  transfers between devices with their start and end apart: 20, of which 10 were waited for; matrix products, arithmetic and copies ran while one was open for 61% of the time, Pallas kernels for 0%

commit v1 on v0

v1 whole, which is shorter than its diff:
```python
import functools

import jax
import jax.numpy as jnp
from jax import lax
from jax.experimental import pallas as pl
from jax.experimental.pallas import tpu as pltpu
from jax.sharding import PartitionSpec as P

HEADS = 8
EPSILON = 1e-05
FLOOR = -1e30
LOW = -1e29
LOG2E = 1.4426950408889634
STATS = 16
F32 = jnp.float32
BF16 = jnp.bfloat16
VMEM_LIMIT = 56 * 1024 * 1024
NT = (((1,), (1,)), ((), ()))
TN = (((0,), (0,)), ((), ()))


def dot(left, right, dims=(((1,), (0,)), ((), ()))):
    return lax.dot_general(left, right, dims, preferred_element_type=F32)


def rms_norm(values, gain):
    return values * lax.rsqrt(jnp.mean(values * values, axis=-1, keepdims=True) + EPSILON) * gain


def swiglu(gate_in, up_in):
    return jax.nn.silu(gate_in) * up_in


def angles_for(positions, head_width):
    exponent = jnp.arange(head_width // 2, dtype=F32) * (2.0 / head_width)
    frequency = jnp.power(10000.0, -exponent)
    turned = positions.astype(F32)[:, None] * frequency[None, :]
    return (jnp.cos(turned), jnp.sin(turned))


def rotate(values, cosine, sine):
    rows, width = values.shape
    split = values.reshape(rows, HEADS, width // HEADS)
    middle = split.shape[-1] // 2
    first, second = split[..., :middle], split[..., middle:]
    cos_rows, sin_rows = cosine[:, None, :], sine[:, None, :]
    turned = jnp.concatenate(
        [first * cos_rows - second * sin_rows, second * cos_rows + first * sin_rows], axis=-1
    )
    return turned.reshape(values.shape)


def params(**more):
    return pltpu.CompilerParams(vmem_limit_bytes=VMEM_LIMIT, **more)


def spread(columns, width=128):
    lanes = lax.broadcasted_iota(jnp.int32, (columns[0].shape[0], width), 1)
    result = jnp.zeros((columns[0].shape[0], width), F32)
    for place, column in enumerate(columns):
        result = jnp.where(lanes == place, column, result)
    return result


def columns_of(rows_by_stat):
    count, width = rows_by_stat.shape
    padded = jnp.concatenate([rows_by_stat, jnp.zeros((128 - count, width), F32)], axis=0)
    return padded.T


def mask_kernel(blocks, order_ref, base_ref, index_ref, bits_ref):
    del order_ref
    rows = index_ref.shape[1]
    lanes = lax.broadcasted_iota(jnp.int32, (8, 128), 1)

    def group(g, carry):
        start = pl.multiple_of(g * 8, 8)
        relative = index_ref[0, pl.ds(start, 8), :] - base_ref[0]
        inside = (relative >= 0) & (relative < blocks * 128)
        place = jnp.where(inside, relative & 127, 0)
        bit = jnp.where(inside, lax.shift_left(jnp.ones_like(relative), relative >> 7), 0)
        code = place | (bit << 7)
        word = jnp.zeros((8, 128), jnp.int32)
        for j in range(index_ref.shape[2]):
            one = jnp.broadcast_to(code[:, j : j + 1], (8, 128))
            word = word | jnp.where((one & 127) == lanes, one >> 7, 0)
        bits_ref[0, pl.ds(start, 8), :] = word
        return carry

    lax.fori_loop(0, rows // 8, group, 0)


def mask_bits(order, base, all_index, mem_dev):
    active = order.shape[0]
    _, rows, count = all_index.shape
    return pl.pallas_call(
        functools.partial(mask_kernel, mem_dev // 128),
        grid_spec=pltpu.PrefetchScalarGridSpec(
            num_scalar_prefetch=2,
            grid=(active,),
            in_specs=[pl.BlockSpec((1, rows, count), lambda a, o, b: (o[a], 0, 0))],
            out_specs=pl.BlockSpec((1, rows, 128), lambda a, o, b: (a, 0, 0)),
        ),
        out_shape=jax.ShapeDtypeStruct((active, rows, 128), jnp.int32),
        compiler_params=params(),
        name="mask_bits",
    )(order, base, all_index)


def fill_bias(bits_ref, bias_ref):
    bits = bits_ref[0]
    for b in range(bias_ref.shape[1] // 128):
        bias_ref[:, b * 128 : (b + 1) * 128] = jnp.where(((bits >> b) & 1) != 0, 0.0, FLOOR)


def owner_forward_kernel(scale, order_ref, q_ref, bits_ref, k_ref, v_ref, o_ref, st_ref, bias_ref):
    del order_ref
    fill_bias(bits_ref, bias_ref)
    maxima, sums = [], []
    for h in range(HEADS):
        span = slice(h * 128, (h + 1) * 128)
        scores = dot(q_ref[0, :, span], k_ref[0, :, span], NT) * scale + bias_ref[...]
        top = jnp.maximum(jnp.max(scores, axis=1, keepdims=True), LOW)
        weights = jnp.exp2(scores - top)
        maxima.append(top)
        sums.append(jnp.sum(weights, axis=1, keepdims=True))
        o_ref[0, :, span] = dot(weights.astype(BF16), v_ref[0, :, span]).astype(BF16)
    st_ref[0] = spread(maxima + sums).T[:STATS]


def owner_forward(order, queries, bits, cached_keys, cached_values, scale):
    segments, rows, width = queries.shape
    mem_dev = cached_keys.shape[1]
    active = order.shape[0]
    picked = lambda a, o: (o[a], 0, 0)
    return pl.pallas_call(
        functools.partial(owner_forward_kernel, scale),
        grid_spec=pltpu.PrefetchScalarGridSpec(
            num_scalar_prefetch=1,
            grid=(active,),
            in_specs=[
                pl.BlockSpec((1, rows, width), picked),
                pl.BlockSpec((1, rows, 128), lambda a, o: (a, 0, 0)),
                pl.BlockSpec((1, mem_dev, width), picked),
                pl.BlockSpec((1, mem_dev, width), picked),
            ],
            out_specs=[
                pl.BlockSpec((1, rows, width), picked),
                pl.BlockSpec((1, STATS, rows), picked),
            ],
            scratch_shapes=[pltpu.VMEM((rows, mem_dev), F32)],
        ),
        out_shape=[
            jax.ShapeDtypeStruct((segments, rows, width), BF16),
            jax.ShapeDtypeStruct((segments, STATS, rows), F32),
        ],
        compiler_params=params(),
        name="owner_forward",
    )(order, queries, bits, cached_keys, cached_values)


def owner_backward_kernel(
    scale, order_ref, q_ref, g_ref, st_ref, bits_ref, k_ref, v_ref, dq_ref, bias_ref
):
    del order_ref
    fill_bias(bits_ref, bias_ref)
    stats = columns_of(st_ref[0])
    for h in range(HEADS):
        span = slice(h * 128, (h + 1) * 128)
        scores = dot(q_ref[0, :, span], k_ref[0, :, span], NT) * scale + bias_ref[...]
        weights = jnp.exp2(scores - stats[:, h : h + 1])
        dweights = dot(g_ref[0, :, span], v_ref[0, :, span], NT)
        dscore = weights * (dweights - stats[:, HEADS + h : HEADS + h + 1])
        dq_ref[0, :, span] = (
            dot(dscore.astype(BF16), k_ref[0, :, span]) * (scale / LOG2E)
        ).astype(BF16)


def owner_backward(order, queries, grads, stats, bits, cached_keys, cached_values, scale):
    segments, rows, width = queries.shape
    mem_dev = cached_keys.shape[1]
    active = order.shape[0]
    picked = lambda a, o: (o[a], 0, 0)
    return pl.pallas_call(
        functools.partial(owner_backward_kernel, scale),
        grid_spec=pltpu.PrefetchScalarGridSpec(
            num_scalar_prefetch=1,
            grid=(active,),
            in_specs=[
                pl.BlockSpec((1, rows, width), picked),
                pl.BlockSpec((1, rows, width), picked),
                pl.BlockSpec((1, STATS, rows), picked),
                pl.BlockSpec((1, rows, 128), lambda a, o: (a, 0, 0)),
                pl.BlockSpec((1, mem_dev, width), picked),
                pl.BlockSpec((1, mem_dev, width), picked),
            ],
            out_specs=pl.BlockSpec((1, rows, width), picked),
            scratch_shapes=[pltpu.VMEM((rows, mem_dev), F32)],
        ),
        out_shape=jax.ShapeDtypeStruct((segments, rows, width), BF16),
        compiler_params=params(),
        name="owner_backward",
    )(order, queries, grads, stats, bits, cached_keys, cached_values)


def causal_bias(place_ref, rows, keys):
    row = place_ref[0] * rows + lax.broadcasted_iota(jnp.int32, (rows, keys), 0)
    return jnp.where(lax.broadcasted_iota(jnp.int32, (rows, keys), 1) <= row, 0.0, FLOOR)


def local_forward_kernel(scale, place_ref, q_ref, k_ref, v_ref, o_ref, st_ref):
    bias = causal_bias(place_ref, q_ref.shape[0], k_ref.shape[0])
    maxima, sums = [], []
    for h in range(HEADS):
        span = slice(h * 128, (h + 1) * 128)
        scores = dot(q_ref[:, span], k_ref[:, span], NT) * scale + bias
        top = jnp.max(scores, axis=1, keepdims=True)
        weights = jnp.exp2(scores - top)
        maxima.append(top)
        sums.append(jnp.sum(weights, axis=1, keepdims=True))
        o_ref[:, span] = dot(weights.astype(BF16), v_ref[:, span])
    st_ref[...] = spread(maxima + sums).T[:STATS]


def whole(*shape):
    return pl.BlockSpec(shape, lambda *_: (0,) * len(shape))


def local_forward(place, queries, keys, values, scale):
    rows, width = queries.shape
    length = keys.shape[0]
    return pl.pallas_call(
        functools.partial(local_forward_kernel, scale),
        grid_spec=pltpu.PrefetchScalarGridSpec(
            num_scalar_prefetch=1,
            grid=(1,),
            in_specs=[whole(rows, width), whole(length, width), whole(length, width)],
            out_specs=[whole(rows, width), whole(STATS, rows)],
        ),
        out_shape=[
            jax.ShapeDtypeStruct((rows, width), F32),
            jax.ShapeDtypeStruct((STATS, rows), F32),
        ],
        compiler_params=params(),
        name="local_forward",
    )(place, queries, keys, values)


def local_backward_kernel(
    scale, place_ref, q_ref, g_ref, st_ref, k_ref, v_ref, dq_ref, dk_ref, dv_ref
):
    bias = causal_bias(place_ref, q_ref.shape[0], k_ref.shape[0])
    stats = columns_of(st_ref[...])
    for h in range(HEADS):
        span = slice(h * 128, (h + 1) * 128)
        query, key, grad = q_ref[:, span], k_ref[:, span], g_ref[:, span]
        scores = dot(query, key, NT) * scale + bias
        weights = jnp.exp2(scores - stats[:, h : h + 1])
        dweights = dot(grad, v_ref[:, span], NT)
        dscore = (weights * (dweights - stats[:, HEADS + h : HEADS + h + 1])).astype(BF16)
        dq_ref[:, span] = dot(dscore, key) * (scale / LOG2E)
        dk_ref[:, span] = (dot(dscore, query, TN) * (scale / LOG2E)).astype(BF16)
        dv_ref[:, span] = dot(weights.astype(BF16), grad, TN).astype(BF16)


def local_backward(place, queries, grads, stats, keys, values, scale):
    rows, width = queries.shape
    length = keys.shape[0]
    return pl.pallas_call(
        functools.partial(local_backward_kernel, scale),
        grid_spec=pltpu.PrefetchScalarGridSpec(
            num_scalar_prefetch=1,
            grid=(1,),
            in_specs=[
                whole(rows, width),
                whole(rows, width),
                whole(STATS, rows),
                whole(length, width),
                whole(length, width),
            ],
            out_specs=[whole(rows, width), whole(length, width), whole(length, width)],
        ),
        out_shape=[
            jax.ShapeDtypeStruct((rows, width), F32),
            jax.ShapeDtypeStruct((length, width), BF16),
            jax.ShapeDtypeStruct((length, width), BF16),
        ],
        compiler_params=params(),
        name="local_backward",
    )(place, queries, grads, stats, keys, values)


def per_device(
    tokens,
    cached_keys,
    cached_values,
    knn_index,
    has_memory,
    w_query,
    w_key,
    w_value,
    w_out,
    gain_attn,
    w_gate,
    w_up,
    w_down,
    gain_ffn,
    cotangent,
):
    both = ("seq", "mem")
    gather = functools.partial(lax.all_gather, axis=0, tiled=True)
    scatter = functools.partial(lax.psum_scatter, scatter_dimension=0, tiled=True)
    inputs = tokens[0].astype(F32)
    rows, width = inputs.shape
    hidden_width = w_gate.shape[1]
    head_width = width // HEADS
    scale = head_width ** (-0.5) * LOG2E
    mem_dev = cached_keys.shape[1]
    place = lax.axis_index("seq").astype(jnp.int32)[None]
    base = (lax.axis_index("mem") * mem_dev).astype(jnp.int32)[None]

    gains = jnp.zeros((w_query.shape[0], 128), BF16)
    gains = gains.at[:, 0].set(gain_attn).at[:, 1].set(gain_ffn)
    first_weights = gather(jnp.concatenate([w_query, w_key, w_value, gains], axis=1), both)
    flag_rows = jnp.broadcast_to(has_memory[:, None], (8, 128))
    shared = gather(jnp.concatenate([knn_index[0], flag_rows], axis=0)[None], "mem")
    all_index, flags = shared[:, :rows], shared[:, rows, 0]
    segments = flags.shape[0]
    order = jnp.argsort(jnp.where(flags > 0, 0, 1), stable=True)[: segments // 2].astype(jnp.int32)
    bits = mask_bits(order, base, all_index, mem_dev)

    qkv_weight = first_weights[:, : 3 * width]
    gain_first = first_weights[:, 3 * width].astype(F32)
    gain_second = first_weights[:, 3 * width + 1].astype(F32)
    out_gate_up = gather(jnp.concatenate([w_out, w_gate, w_up], axis=1), both)
    down_weight = gather(w_down, both)
    out_weight = out_gate_up[:, :width]
    gate_weight = out_gate_up[:, width : width + hidden_width]
    up_weight = out_gate_up[:, width + hidden_width :]

    positions = lax.axis_index("seq") * rows + jnp.arange(rows)
    cosine, sine = angles_for(positions, head_width)
    normed_one, norm_one_back = jax.vjp(rms_norm, inputs, gain_first)
    norm_one = normed_one.astype(BF16)
    qkv = dot(norm_one, qkv_weight)
    queries = rotate(qkv[:, :width], cosine, sine).astype(BF16)
    keys = rotate(qkv[:, width : 2 * width], cosine, sine).astype(BF16)
    values = qkv[:, 2 * width :].astype(BF16)
    all_queries = gather(queries[None], "mem")
    segment_keys, segment_values = gather(keys, "seq"), gather(values, "seq")

    owner_out, owner_stats = owner_forward(
        order, all_queries, bits, cached_keys, cached_values, scale
    )
    local_out, local_stats = local_forward(place, queries, segment_keys, segment_values, scale)
    exchange = functools.partial(
        lax.all_to_all, axis_name="mem", split_axis=0, concat_axis=0, tiled=True
    )
    peer_out, peer_stats = exchange(owner_out), exchange(owner_stats)
    live = has_memory[0] > 0
    peer_max = jnp.where(live, peer_stats[:, :HEADS], LOW)
    peer_sum = jnp.where(live, peer_stats[:, HEADS:], 0.0)
    local_max, local_sum = local_stats[:HEADS], local_stats[HEADS:]
    row_max = jnp.maximum(local_max, jnp.max(peer_max, axis=0))
    peer_share = jnp.exp2(peer_max - row_max)
    local_share = jnp.exp2(local_max - row_max)
    row_sum = local_sum * local_share + jnp.sum(peer_sum * peer_share, axis=0)
    log_total = row_max + jnp.log2(row_sum)

    def wide(stat):
        return jnp.broadcast_to(
            jnp.swapaxes(stat, -1, -2)[..., None], stat.shape[:-2] + (rows, HEADS, head_width)
        ).reshape(stat.shape[:-2] + (rows, width))

    peer_sums = jnp.sum(
        jnp.where(live, peer_out.astype(F32), 0.0) * wide(peer_share / row_sum), axis=0
    )
    attention = local_out * wide(local_share / row_sum) + peer_sums
    attention_low = attention.astype(BF16)
    mid = inputs + dot(attention_low, out_weight)
    normed_two, norm_two_back = jax.vjp(rms_norm, mid, gain_second)
    norm_two = normed_two.astype(BF16)
    gate = dot(norm_two, gate_weight)
    upward = dot(norm_two, up_weight)
    gated, gated_back = jax.vjp(swiglu, gate, upward)
    hidden = gated.astype(BF16)
    mixed = mid + dot(hidden, down_weight)
    grad_out = cotangent[0]
    grad_hidden = dot(grad_out, down_weight, NT)
    grad_gate_full, grad_up_full = gated_back(grad_hidden)
    grad_gate, grad_upward = grad_gate_full.astype(BF16), grad_up_full.astype(BF16)
    grad_norm_two = dot(grad_gate, gate_weight, NT) + dot(grad_upward, up_weight, NT)
    grad_mid_norm, grad_gain_second = norm_two_back(grad_norm_two)
    grad_mid = grad_out.astype(F32) + grad_mid_norm
    grad_mid_low = grad_mid.astype(BF16)
    grad_attention = dot(grad_mid_low, out_weight, NT).astype(BF16)
    grad_dots = jnp.sum(
        (grad_attention.astype(F32) * attention).reshape(rows, HEADS, head_width), axis=2
    ).T
    back_stats = jnp.concatenate([log_total, grad_dots], axis=0)
    all_grads, all_stats = gather(grad_attention[None], "mem"), gather(back_stats[None], "mem")

    early = jnp.concatenate(
        [
            dot(attention_low, grad_mid_low, TN),
            dot(norm_two, grad_gate, TN),
            dot(norm_two, grad_upward, TN),
        ],
        axis=1,
    ).astype(BF16)
    early_sum = scatter(early, both)
    down_sum = scatter(dot(hidden, grad_out, TN).astype(BF16), both)

    local_dq, local_dk, local_dv = local_backward(
        place, queries, grad_attention, back_stats, segment_keys, segment_values, scale
    )
    owner_grads = owner_backward(
        order, all_queries, all_grads, all_stats, bits, cached_keys, cached_values, scale
    )
    peer_grads = exchange(owner_grads)
    grad_queries = local_dq + jnp.sum(jnp.where(live, peer_grads.astype(F32), 0.0), axis=0)
    grad_keys_mine = scatter(local_dk, "seq").astype(F32)
    grad_value_in = scatter(local_dv, "seq")
    grad_query_in = rotate(grad_queries, cosine, -sine).astype(BF16)
    grad_key_in = rotate(grad_keys_mine, cosine, -sine).astype(BF16)
    grad_in = jnp.concatenate([grad_query_in, grad_key_in, grad_value_in], axis=1)
    grad_norm_one = dot(grad_in, qkv_weight, NT)
    grad_in_norm, grad_gain_first = norm_one_back(grad_norm_one)
    grad_inputs = grad_mid + grad_in_norm
    late = jnp.concatenate(
        [
            dot(norm_one, grad_in, TN).astype(BF16),
            jnp.zeros((width, 128), BF16)
            .at[:, 0]
            .set(grad_gain_first.astype(BF16))
            .at[:, 1]
            .set(grad_gain_second.astype(BF16)),
        ],
        axis=1,
    )
    late_sum = scatter(late, both).astype(F32)
    early_sum = early_sum.astype(F32)
    return (
        mixed[None],
        grad_inputs[None],
        late_sum[:, :width],
        late_sum[:, width : 2 * width],
        late_sum[:, 2 * width : 3 * width],
        early_sum[:, :width],
        late_sum[:, 3 * width],
        early_sum[:, width : width + hidden_width],
        early_sum[:, width + hidden_width :],
        down_sum.astype(F32),
        late_sum[:, 3 * width + 1],
    )


def solution(mesh):
    rows, owned, feature = P("mem", "seq", None), P(None, "mem", None), P(("seq", "mem"), None)
    gain = P(("seq", "mem"))
    return jax.shard_map(
        per_device,
        mesh=mesh,
        in_specs=(
            (rows, owned, owned, rows, P("mem"))
            + (feature,) * 4
            + (gain,)
            + (feature,) * 3
            + (gain, rows)
        ),
        out_specs=(rows, rows) + (feature,) * 4 + (gain,) + (feature,) * 3 + (gain,),
        check_vma=False,
    )
```

time: 2700 us -> 1080 us (0.40)
  local copies, waits for them, and re-layouts: 1330 us -> 41 us
  matrix products: 310 us -> 53.8 us
  waiting for transfers between devices: 863 us -> 757 us
  Pallas kernels: 0 us -> 101 us
  blocking collectives: 71.2 us -> 25.1 us
    while x18 -> x0, local copies, waits for them, and re-layouts: 1120 us -> none
    dot_general x93 -> x15, matrix products: 310 us -> 53.8 us  [dot(): return lax.dot_general(left, right, dims, preferred_element_type=F32)]
    reduce_scatter x4 -> x5, waiting for transfers between devices: 591 us -> 368 us  [the longest x1 163 us: per_device(): early_sum = scatter(early, both)]
    all_gather x12 -> x8, waiting for transfers between devices: 141 us -> 275 us  [the longest x1 73 us: per_device(): out_gate_up = gather(jnp.concatenate([w_out, w_gate, w_up], axis=1), both)]
    dynamic_slice x96 -> x0, local copies, waits for them, and re-layouts: 102 us -> none  [the longest x56 87.4 us: per_device(): lax.map(owner_scores, (all_queries, all_index, cached_keys))]
    pallas_call x0 -> x5, Pallas kernels: none -> 101 us  [the longest x1 40.9 us: mask_bits(): pl.pallas_call(functools.partial(mask_kernel, mem_dev // 128), grid_spec=...]
    unnamed x1 -> x0, blocking collectives: 42.9 us -> none
    concatenate x1 -> x2, local copies, waits for them, and re-layouts: 42.6 us -> 2.65 us  [the longest x1 1.57 us: per_device(): jnp.concatenate([knn_index[0], flag_rows], axis=0)[None]]
  transfers between devices with their start and end apart: 20 -> 15, of which waited for: 10 -> 11; matrix products, arithmetic and copies ran while one was open for 61% -> 11% of each run, Pallas kernels for 0% -> 9%
where the time goes in v1:
time: 1080 us; the launch traced here: 1070 us
  waiting for transfers between devices  757 us (70%)
  Pallas kernels  101 us (9%)
  matrix products  53.8 us (5%)
  other arithmetic  50.1 us (5%)
  local copies, waits for them, and re-layouts  41 us (4%)
  blocking collectives  25.1 us (2%)
  starting transfers between devices  21.8 us (2%)
  between operations  15.4 us (1%)
    reduce_scatter x1, waiting for transfers between devices, per_device(): early_sum = scatter(early, both)  163 us
    reduce_scatter x1, waiting for transfers between devices, per_device(): late_sum = scatter(late, both).astype(F32)  145 us
    all_to_all x1, waiting for transfers between devices, per_device(): peer_grads = exchange(owner_grads)  113 us
    all_gather x1, waiting for transfers between devices, per_device(): out_gate_up = gather(jnp.concatenate([w_out, w_gate, w_up], axis=1), both)  73 us
    all_gather x2, waiting for transfers between devices, per_device(): segment_keys, segment_values = (gather(keys, 'seq'), gather(values, 'seq'))  72.1 us
    all_gather x1, waiting for transfers between devices, per_device(): gather(jnp.concatenate([w_query, w_key, w_value, gains], axis=1), both)  68.8 us
    reduce_scatter x1, waiting for transfers between devices, per_device(): down_sum = scatter(dot(hidden, grad_out, TN).astype(BF16), both)  60.3 us
    dot_general x15, matrix products, dot(): return lax.dot_general(left, right, dims, preferred_element_type=F32)  53.8 us
  transfers between devices with their start and end apart: 15, of which 11 were waited for; matrix products, arithmetic and copies ran while one was open for 11% of the time, Pallas kernels for 9%

profile of v1, /device:TPU:0, one launch (start us, length us, event | category | flops | bytes accessed | tf_op | source)
XLA Modules:
  0.0 1065.6 jit_solution(11780040400713475579)
XLA Ops:
  17.6 68.8 %all-gather.12.cloned.1.call-done = bf16[1024,3200]{1,0:T(8,128)(2,1)} async-done(((bf16[32,3200]{1,0:T(8,128)(2,1)}), bf16[1024,3200]{1,0:T(8,128)(2,1)}) %all-gather.12.cloned.1.call-update) | async-done | bytes 6553616 | tf_op jit(solution)/shard_map/all_gather | solution.py:325
  87.8 4.8 fusion.2
  101.3 8.2 all-gather.24.cloned.1.call-done
  113.7 40.9 %mask_bits.1.bits_ref = s32[4,256,128]{2,1,0:T(8,128)} custom-call(s32[4]{0:T(128)} %bitcast.108, s32[1]{0:T(128)} %bitcast.8.base_ref, s32[8,256,128]{2,1,0:T(8,128)} %slice.197.index_ref), custom_call_target="tpu_custom_call" | custom-call | tf_op jit(solution)/shard_map/mask_bits/pallas_call | solution.py:97
  154.6 4.4 all-gather.18.cloned.1.call-done.q_ref
  159.0 20.7 %owner_forward.1 = (bf16[8,256,1024]{2,1,0:T(8,128)(2,1)}, f32[8,16,256]{2,1,0:T(8,128)}) custom-call(s32[4]{0:T(128)} %bitcast.109, bf16[8,256,1024]{2,1,0:T(8,128)(2,1)} %all-gather.18.cloned.1.call-done.q_ref, s32[4,256,128]{2,1,0:T(8,128)} %mask_bits.1.bits_ref, bf16[8,1024,1024]{2,1,0:T(8,128)(2,1)} %k_ref.3, bf16[8,1024,1024]{2,1,0:T(8,128)(2,1)} %v_ref.3), custom_call_target="tpu_custom_call" | custom-call | tf_op jit(solution)/shard_map/owner_forward/pallas_call | solution.py:137
  179.7 10.1 all_to_all.15
  189.8 4.7 all-to-all-start.1
  194.5 11.3 %all-gather.26.cloned.1.call-start = ((), (), s32[]{:S(2)}) async-start(), calls=%async_computation.20 | async-start | bytes 4718592 | tf_op jit(solution)/shard_map/all_gather | solution.py:402
  205.8 48.6 %all-gather.22.cloned.1.call-done = bf16[2816,1024]{1,0:T(8,128)(2,1)} async-done(((bf16[88,1024]{1,0:T(8,128)(2,1)}), bf16[2816,1024]{1,0:T(8,128)(2,1)}) %all-gather.22.cloned.1.call-update) | async-done | bytes 5767184 | tf_op jit(solution)/shard_map/all_gather | solution.py:337
  254.4 5.9 fusion.40
  261.1 35.1 %all-gather.14.cloned.1.call-done.k_ref = bf16[1024,1024]{1,0:T(8,128)(2,1)} async-done(((bf16[256,1024]{1,0:T(8,128)(2,1)}), bf16[1024,1024]{1,0:T(8,128)(2,1)}) %all-gather.14.cloned.1.call-update) | async-done | bytes 2097168 | tf_op jit(solution)/shard_map/all_gather | solution.py:351
  296.2 37.0 %all-gather.16.cloned.1.call-done.v_ref = bf16[1024,1024]{1,0:T(8,128)(2,1)} async-done(((bf16[256,1024]{1,0:T(8,128)(2,1)}), bf16[1024,1024]{1,0:T(8,128)(2,1)}) %all-gather.16.cloned.1.call-update) | async-done | bytes 2097168 | tf_op jit(solution)/shard_map/all_gather | solution.py:351
  333.3 7.6 local_forward.1
  342.7 4.7 broadcast_in_dim.88
  347.5 9.3 reshape.339
  356.9 6.2 multiply_reduce_fusion
  363.9 73.0 %all-gather.20.cloned.1.call-done = bf16[1024,6656]{1,0:T(8,128)(2,1)} async-done(((bf16[32,6656]{1,0:T(8,128)(2,1)}), bf16[1024,6656]{1,0:T(8,128)(2,1)}) %all-gather.20.cloned.1.call-update) | async-done | bytes 13631504 | tf_op jit(solution)/shard_map/all_gather | solution.py:336
  439.7 5.5 fusion.6
  445.8 4.1 fusion.14
  458.0 11.1 %local_backward.1 = (f32[256,1024]{1,0:T(8,128)}, bf16[1024,1024]{1,0:T(8,128)(2,1)}, bf16[1024,1024]{1,0:T(8,128)(2,1)}) custom-call(s32[1]{0:T(128)} %bitcast.1.place_ref, bf16[256,1024]{1,0:T(8,128)(2,1)} %bitcast.95, bf16[256,1024]{1,0:T(8,128)(2,1)} %fusion.26.g_ref, f32[16,256]{1,0:T(8,128)} %pad_maximum_fusion.7.st_ref, ...), custom_call_target="tpu_custom_call" | custom-call | tf_op jit(solution)/shard_map/local_backward/pallas_call | solution.py:270
  469.8 5.2 convolution_convert_fusion
  485.7 10.2 pad_maximum_fusion
  496.6 15.0 %all-gather.2 = f32[128,256]{1,0:T(8,128)} all-gather(f32[16,256]{1,0:T(8,128)S(1)} %copy-done.19), channel_id=4, replica_groups=mesh['seq'=4,'mem'=8] {'mem'}, dimensions={0}, use_global_device_ids=true | all-gather | bytes 147456 | tf_op jit(solution)/shard_map/all_gather | solution.py:402
  511.7 20.9 %owner_backward.1 = bf16[8,256,1024]{2,1,0:T(8,128)(2,1)} custom-call(s32[4]{0:T(128)} %bitcast.110, bf16[8,256,1024]{2,1,0:T(8,128)(2,1)} %all-gather.18.cloned.1.call-done.q_ref, bf16[8,256,1024]{2,1,0:T(8,128)(2,1)} %bitcast.96, f32[8,16,256]{2,1,0:T(8,128)} %bitcast.105, s32[4,256,128]{2,1,0:T(8,128)} %mask_bits.1.bits_ref, ...), custom_call_target="tpu_custom_call" | custom-call | tf_op jit(solution)/shard_map/owner_backward/pallas_call | solution.py:185
  532.6 4.6 all-to-all-start.2
  540.4 112.7 %all-to-all-done.2 = bf16[8,256,1024]{2,1,0:T(8,128)(2,1)} async-done(((bf16[8,256,1024]{2,1,0:T(8,128)(2,1)}), bf16[8,256,1024]{2,1,0:T(8,128)(2,1)}, u32[]{:S(2)}, u32[]{:S(2)}) %all-to-all-start.2) | async-done | bytes 4194336 | tf_op jit(solution)/shard_map/all_to_all | solution.py:421
  659.4 5.8 fusion.32
  674.2 5.7 fusion.25
  679.9 60.3 %reduce-scatter.14.cloned.1.call-done = bf16[88,1024]{1,0:T(8,128)(2,1)} async-done(((bf16[2816,1024]{1,0:T(8,128)(2,1)}), bf16[88,1024]{1,0:T(8,128)(2,1)}) %reduce-scatter.14.cloned.1.call-update) | async-done | bytes 180240 | tf_op jit(solution)/shard_map/reduce_scatter | solution.py:413
  744.3 162.9 %reduce-scatter.12.cloned.1.call-done = bf16[32,6656]{1,0:T(8,128)(2,1)} async-done(((bf16[1024,6656]{1,0:T(8,128)(2,1)}), bf16[32,6656]{1,0:T(8,128)(2,1)}) %reduce-scatter.12.cloned.1.call-update) | async-done | bytes 426000 | tf_op jit(solution)/shard_map/reduce_scatter | solution.py:412
  910.6 144.9 %reduce-scatter.10.cloned.1.call-done = bf16[32,3200]{1,0:T(8,128)(2,1)} async-done(((bf16[1024,3200]{1,0:T(8,128)(2,1)}), bf16[32,3200]{1,0:T(8,128)(2,1)}) %reduce-scatter.10.cloned.1.call-update) | async-done | bytes 204816 | tf_op jit(solution)/shard_map/reduce_scatter | solution.py:442
  (161 shorter events, 80.0 us)
Async XLA Ops:
  7.2 79.2 %all-gather.12.cloned.1.call-start = ((), (), s32[]{:S(2)}) async-start(), calls=%async_computation.8 | async-start | bytes 6758400 | tf_op jit(solution)/shard_map/all_gather | solution.py:325
  12.8 96.7 %all-gather.24.cloned.1.call-start = ((), (), s32[]{:S(2)}) async-start(), calls=%async_computation.19 | async-start | bytes 1216512 | tf_op jit(solution)/shard_map/all_gather | solution.py:327
  15.1 143.9 %all-gather.18.cloned.1.call-start = ((), (), s32[]{:S(2)}) async-start(), calls=%async_computation.11 | async-start | bytes 4718592 | tf_op jit(solution)/shard_map/all_gather | solution.py:350
  17.6 78.9 %copy-start.8 = (f32[256,64]{1,0:T(8,128)}, f32[256,64]{1,0:T(8,128)S(1)}, u32[]{:S(2)}) copy-start(f32[256,64]{1,0:T(8,128)S(1)} %get-tuple-element.107) | copy-start | bytes 196612
  95.6 158.8 %all-gather.22.cloned.1.call-start = ((), (), s32[]{:S(2)}) async-start(), calls=%async_computation.13 | async-start | bytes 5947392 | tf_op jit(solution)/shard_map/all_gather | solution.py:337
  96.2 200.1 %all-gather.14.cloned.1.call-start = ((), (), s32[]{:S(2)}) async-start(), calls=%async_computation.9 | async-start | bytes 2621440 | tf_op jit(solution)/shard_map/all_gather | solution.py:351
  96.4 4.0 copy-start.17
  96.4 4.0 copy-start.18
  96.4 4.0 copy-start.21
  98.2 235.1 %all-gather.16.cloned.1.call-start = ((), (), s32[]{:S(2)}) async-start(), calls=%async_computation.10 | async-start | bytes 2621440 | tf_op jit(solution)/shard_map/all_gather | solution.py:351
  100.4 336.6 %all-gather.20.cloned.1.call-start = ((), (), s32[]{:S(2)}) async-start(), calls=%async_computation.12 | async-start | bytes 14057472 | tf_op jit(solution)/shard_map/all_gather | solution.py:336
  189.8 64.6 %copy-start.10 = (bf16[1,256,1024]{2,1,0:T(8,128)(2,1)S(1)}, bf16[1,256,1024]{2,1,0:T(8,128)(2,1)}, u32[]{:S(2)}) copy-start(bf16[1,256,1024]{2,1,0:T(8,128)(2,1)} %param.37) | copy-start | bytes 1572868
  189.8 167.2 %all-to-all-start.1 = ((bf16[8,256,1024]{2,1,0:T(8,128)(2,1)}), bf16[8,256,1024]{2,1,0:T(8,128)(2,1)}, u32[]{:S(2)}, u32[]{:S(2)}) async-start(bf16[8,256,1024]{2,1,0:T(8,128)(2,1)} %get-tuple-element.71), calls=%async_computation.1 | async-start | bytes 8388608 | tf_op jit(solution)/shard_map/all_to_all | solution.py:360
  194.5 317.2 %all-gather.26.cloned.1.call-start = ((), (), s32[]{:S(2)}) async-start(), calls=%async_computation.20 | async-start | bytes 4718592 | tf_op jit(solution)/shard_map/all_gather | solution.py:402
  347.5 9.3 copy-start.20
  356.9 6.5 copy-start.15
  363.1 73.8 %copy-start.2 = (bf16[1,256,1024]{2,1,0:T(8,128)(2,1)S(1)}, bf16[1,256,1024]{2,1,0:T(8,128)(2,1)}, u32[]{:S(2)}) copy-start(bf16[1,256,1024]{2,1,0:T(8,128)(2,1)} %param.23) | copy-start | bytes 1572868
  436.9 8.3 copy-start.22
  439.5 13.9 %copy-start.4 = (f32[256,1024]{1,0:T(8,128)}, f32[256,1024]{1,0:T(8,128)S(1)}, u32[]{:S(2)}) copy-start(f32[256,1024]{1,0:T(8,128)S(1)} %get-tuple-element.109) | copy-start | bytes 3145732
  439.7 5.6 copy-start
  439.7 6.1 copy-start.23
  455.3 83.6 %reduce-scatter.6.cloned.1.call-start = ((), (), s32[]{:S(2)}) async-start(), calls=%async_computation.14 | async-start | bytes 2621440 | tf_op jit(solution)/shard_map/reduce_scatter | solution.py:423
  458.0 11.8 %copy-start.6 = (bf16[256,2816]{1,0:T(8,128)(2,1)S(1)}, bf16[256,2816]{1,0:T(8,128)(2,1)}, u32[]{:S(2)}) copy-start(bf16[256,2816]{1,0:T(8,128)(2,1)} %get-tuple-element.87) | copy-start | bytes 4325380
  469.2 189.1 %reduce-scatter.8.cloned.1.call-start = ((), (), s32[]{:S(2)}) async-start(), calls=%async_computation.15 | async-start | bytes 2621440 | tf_op jit(solution)/shard_map/reduce_scatter | solution.py:424
  469.8 270.4 %reduce-scatter.14.cloned.1.call-start = ((), (), s32[]{:S(2)}) async-start(), calls=%async_computation.18 | async-start | bytes 5947392 | tf_op jit(solution)/shard_map/reduce_scatter | solution.py:413
  475.1 432.2 %reduce-scatter.12.cloned.1.call-start = ((), (), s32[]{:S(2)}) async-start(), calls=%async_computation.17 | async-start | bytes 14057472 | tf_op jit(solution)/shard_map/reduce_scatter | solution.py:412
  480.5 3.5 copy-start.1
  532.6 120.5 %all-to-all-start.2 = ((bf16[8,256,1024]{2,1,0:T(8,128)(2,1)}), bf16[8,256,1024]{2,1,0:T(8,128)(2,1)}, u32[]{:S(2)}, u32[]{:S(2)}) async-start(bf16[8,256,1024]{2,1,0:T(8,128)(2,1)} %owner_backward.1), calls=%async_computation.2 | async-start | bytes 8388608 | tf_op jit(solution)/shard_map/all_to_all | solution.py:421
  537.2 518.4 %reduce-scatter.10.cloned.1.call-start = ((), (), s32[]{:S(2)}) async-start(), calls=%async_computation.16 | async-start | bytes 6758400 | tf_op jit(solution)/shard_map/reduce_scatter | solution.py:442
  538.9 117.5 %copy-start.14 = (f32[256,1024]{1,0:T(8,128)S(1)}, f32[256,1024]{1,0:T(8,128)}, u32[]{:S(2)}) copy-start(f32[256,1024]{1,0:T(8,128)} %get-tuple-element.72) | copy-start | bytes 3145732
  540.3 116.4 %copy-start.9 = (f32[256,64]{1,0:T(8,128)S(1)}, f32[256,64]{1,0:T(8,128)}, u32[]{:S(2)}) copy-start(f32[256,64]{1,0:T(8,128)} %copy-done.8) | copy-start | bytes 196612
  540.3 116.4 %copy-start.16 = (f32[256,64]{1,0:T(8,128)S(1)}, f32[256,64]{1,0:T(8,128)}, u32[]{:S(2)}) copy-start(f32[256,64]{1,0:T(8,128)} %get-tuple-element.105) | copy-start | bytes 196612
  (7 other events, 12.3 us)
Sparse Core Ops, SparseCore 0:
  12.9 73.4 all-gather.11
  88.6 20.7 all-gather.23
  111.6 47.3 all-gather.17
  161.7 92.5 all-gather.21
  256.0 40.1 all-gather.13
  297.9 35.2 all-gather.15
  336.1 100.7 all-gather.19
  455.4 45.2 all-gather.25
  503.8 33.9 reduce-scatter.5
  540.8 35.2 reduce-scatter.7
  578.3 161.7 reduce-scatter.13
  742.3 164.8 reduce-scatter.11
  909.5 146.0 reduce-scatter.9

commit v2 on v1

--- a/solution.py
+++ b/solution.py
@@ -13,6 +13,7 @@
 LOW = -1e29
 LOG2E = 1.4426950408889634
 STATS = 16
+PIECES = 4
 F32 = jnp.float32
 BF16 = jnp.bfloat16
 VMEM_LIMIT = 56 * 1024 * 1024
@@ -67,6 +68,525 @@
     count, width = rows_by_stat.shape
     padded = jnp.concatenate([rows_by_stat, jnp.zeros((128 - count, width), F32)], axis=0)
     return padded.T
+
+
+MESH = pl.DeviceIdType.MESH
+
+
+class Net:
+    def __init__(self, line):
+        self.line = line
+        self.s, self.m = lax.axis_index("seq"), lax.axis_index("mem")
+        self.c, self.z = self.m % 2, self.m // 2
+        self.x, self.y, self.core = (self.s ^ 1, self.m), (self.s ^ 2, self.m), (self.s, self.m ^ 1)
+        self.right = (self.s, (self.m + 2) % (2 * line))
+        self.left = (self.s, (self.m + 2 * line - 2) % (2 * line))
+
+    def greet(self, others):
+        barrier = pltpu.get_barrier_semaphore()
+        for other in others:
+            pl.semaphore_signal(barrier, inc=1, device_id=other, device_id_type=MESH)
+        pl.semaphore_wait(barrier, len(others))
+
+
+def remote(src, dst, sends, recvs, place, device):
+    return pltpu.make_async_remote_copy(
+        src_ref=src,
+        dst_ref=dst,
+        send_sem=sends.at[place],
+        recv_sem=recvs.at[place],
+        device_id=device,
+        device_id_type=MESH,
+    )
+
+
+def row_halves(ref, part):
+    half = ref.shape[-2] // 2
+    return ref.at[pl.ds(part * half, half)]
+
+
+def column_halves(ref, part):
+    half = ref.shape[-1] // 2
+    return ref.at[:, pl.ds(part * half, half)]
+
+
+class Gather:
+    def __init__(self, net, src, out, sends, recvs, own, index, halves, line=True, square=True, core=True):
+        self.net, self.src, self.out, self.sends, self.recvs, self.own = net, src, out, sends, recvs, own
+        self.index, self.halves = index, halves
+        self.line, self.square, self.core = line, square, core
+
+    def slot(self, s, z):
+        return self.out.at[self.index(s, z, self.net.c)]
+
+    def send(self, block, target, place, device):
+        copy = remote(block, target, self.sends, self.recvs, place, device)
+        copy.start()
+
+    def sent(self, block, place):
+        remote(block, block, self.sends, self.recvs, place, self.net.core).wait_send()
+
+    def arrived(self, block, place):
+        remote(block, block, self.sends, self.recvs, place, self.net.core).wait_recv()
+
+    def places(self):
+        z = self.net.line
+        right, left, square, core = 0, z, 2 * z, 8 * z
+        return right, left, square, core
+
+    def steps(self, body):
+        net = self.net
+        body(0, net.z, None)
+        if self.line:
+            for k in range(1, net.line):
+                self.step(k, body)
+
+    def step(self, k, body):
+        net = self.net
+        if k == 0:
+            body(0, net.z, None)
+            return
+        if not self.line:
+            return
+        pl.when(net.z >= k)(lambda: body(k, net.z - k, True))
+        pl.when(net.z + k < net.line)(lambda: body(k, net.z + k, False))
+
+    def have(self, k, z, from_left):
+        net = self.net
+        right, left, square, core = self.places()
+        target = self.slot(net.s, z)
+        block = self.src if k == 0 else target
+        if k == 0:
+            pltpu.make_async_copy(self.src, target, self.own).start()
+        else:
+            self.arrived(target, (right if from_left else left) + z)
+        if self.line:
+            if from_left is not False:
+                pl.when(net.z < net.line - 1)(lambda: self.send(block, target, right + z, net.right))
+            if from_left is not True:
+                pl.when(net.z > 0)(lambda: self.send(block, target, left + z, net.left))
+        if self.square:
+            for kind, part, device in ((0, 0, net.x), (2, 1, net.y), (1, 0, net.y), (3, 1, net.x)):
+                self.send(
+                    self.halves(block, part),
+                    self.halves(target, part),
+                    square + kind * net.line + z,
+                    device,
+                )
+        if self.core:
+            self.send(block, target, core + z, net.core)
+
+    def pass_square(self, k, z, from_left):
+        net = self.net
+        _, _, square, core = self.places()
+        for kind, part, other, then, device, mirror in (
+            (0, 0, net.s ^ 1, 4, net.y, 1),
+            (2, 1, net.s ^ 2, 5, net.x, 2),
+        ):
+            block = self.halves(self.slot(other, z), part)
+            self.arrived(block, square + kind * net.line + z)
+            self.send(block, block, square + then * net.line + z, device)
+            if self.core:
+                self.send(block, block, core + mirror * net.line + z, net.core)
+
+    def end_square(self, k, z, from_left):
+        net = self.net
+        _, _, square, core = self.places()
+        for kind, part, other, mirror in self.last(net):
+            block = self.halves(self.slot(other, z), part)
+            self.arrived(block, square + kind * net.line + z)
+            if self.core:
+                self.send(block, block, core + mirror * net.line + z, net.core)
+
+    def last(self, net):
+        return (
+            (1, 0, net.s ^ 2, 3),
+            (3, 1, net.s ^ 1, 5),
+            (4, 0, net.s ^ 3, 4),
+            (5, 1, net.s ^ 3, 6),
+        )
+
+    def finish(self):
+        net = self.net
+        right, left, square, core = self.places()
+        own = self.slot(net.s, net.z)
+        pltpu.make_async_copy(self.src, own, self.own).wait()
+        if self.core:
+            for z in range(net.line if self.line else 1):
+                z = z if self.line else net.z
+                for mirror, part, other in (
+                    (0, None, net.s),
+                    (1, 0, net.s ^ 1),
+                    (2, 1, net.s ^ 2),
+                    (3, 0, net.s ^ 2),
+                    (4, 0, net.s ^ 3),
+                    (5, 1, net.s ^ 1),
+                    (6, 1, net.s ^ 3),
+                ):
+                    if part is not None and not self.square:
+                        continue
+                    block = self.out.at[self.index(other, z, 1 - net.c)]
+                    block = block if part is None else self.halves(block, part)
+                    self.arrived(block, core + mirror * net.line + z)
+                    self.sent(block, core + mirror * net.line + z)
+        if self.square:
+            half = [self.halves(own, 0), self.halves(own, 1)]
+            for z in range(net.line if self.line else 1):
+                z = z if self.line else net.z
+                for kind, part in ((0, 0), (1, 0), (2, 1), (3, 1), (4, 0), (5, 1)):
+                    self.sent(half[part], square + kind * net.line + z)
+        if self.line:
+            for z in range(net.line):
+                pl.when((z <= net.z) & (net.z < net.line - 1))(lambda z=z: self.sent(own, right + z))
+                pl.when((z >= net.z) & (net.z > 0))(lambda z=z: self.sent(own, left + z))
+
+
+def run_gathers(gathers, line):
+    for k in range(line):
+        for gather in gathers:
+            gather.step(k, gather.have)
+        if k > 0:
+            for gather in gathers:
+                if gather.square:
+                    gather.step(k - 1, gather.pass_square)
+    for gather in gathers:
+        if gather.square:
+            gather.step(line - 1, gather.pass_square)
+    for k in range(line):
+        for gather in gathers:
+            if gather.square:
+                gather.step(k, gather.end_square)
+    for gather in gathers:
+        gather.finish()
+
+
+def gather_kernel(line, plan, *refs):
+    count = len(plan)
+    sources, outs, sems = refs[:count], refs[count : 2 * count], refs[2 * count :]
+    net = Net(line)
+    net.greet([net.x, net.y, net.core, net.left, net.right])
+    index = {
+        "all": lambda s, z, c: (s * line + z) * 2 + c,
+        "line": lambda s, z, c: z * 2 + c,
+        "square": lambda s, z, c: s,
+    }
+    gathers = []
+    for i, (halves, reach) in enumerate(plan):
+        sends, recvs, own = sems[3 * i : 3 * i + 3]
+        gathers.append(
+            Gather(
+                net,
+                sources[i],
+                outs[i],
+                sends,
+                recvs,
+                own,
+                index[reach],
+                halves,
+                line=reach != "square",
+                square=reach != "line",
+                core=reach != "square",
+            )
+        )
+    run_gathers(gathers, line)
+
+
+def gather_many(collective_id, name, sizes, arrays, plan):
+    line = sizes["mem"] // 2
+    slots = {"all": sizes["seq"] * sizes["mem"], "line": sizes["mem"], "square": sizes["seq"]}
+    anywhere = pl.BlockSpec(memory_space=pl.ANY)
+    scratch = []
+    for _ in plan:
+        scratch += [pltpu.SemaphoreType.DMA((15 * line,))] * 2 + [pltpu.SemaphoreType.DMA]
+    moved = sum(a.size * a.dtype.itemsize * slots[reach] for a, (_, reach) in zip(arrays, plan))
+    return pl.pallas_call(
+        functools.partial(gather_kernel, line, plan),
+        out_shape=[
+            jax.ShapeDtypeStruct((slots[reach],) + a.shape, a.dtype)
+            for a, (_, reach) in zip(arrays, plan)
+        ],
+        in_specs=[anywhere] * len(plan),
+        out_specs=[anywhere] * len(plan),
+        scratch_shapes=scratch,
+        compiler_params=params(collective_id=collective_id, has_side_effects=True),
+        cost_estimate=pl.CostEstimate(flops=0, bytes_accessed=2 * moved, transcendentals=0),
+        name=name,
+    )(*arrays)
+
+
+class Scatter:
+    def __init__(self, net, src, out, buffers, sems, halves, whole=True):
+        self.net, self.src, self.out, self.halves = net, src, out, halves
+        self.whole, self.count = whole, src.shape[1]
+        self.held, self.twin, self.first, self.second, self.along = buffers
+        self.sends, self.recvs, self.own = sems
+
+    def send(self, block, target, place, device):
+        remote(block, target, self.sends, self.recvs, place, device).start()
+
+    def sent(self, block, place):
+        remote(block, block, self.sends, self.recvs, place, self.net.core).wait_send()
+
+    def arrived(self, block, place):
+        remote(block, block, self.sends, self.recvs, place, self.net.core).wait_recv()
+
+    def places(self):
+        z = self.count
+        return 0, 4 * z, 8 * z, 10 * z, 11 * z
+
+    def loading(self, d):
+        source = self.src.at[:, d, self.net.c] if self.whole else self.src.at[:, d]
+        return pltpu.make_async_copy(source, self.held.at[:, d], self.own.at[d])
+
+    def load(self, d):
+        net = self.net
+        self.loading(d).start()
+        for s in range(4 if self.whole else 0):
+            self.send(self.src.at[s, d, 1 - net.c], self.twin.at[s, d], s * self.count + d, net.core)
+
+    def add_core(self, d):
+        net = self.net
+        _, first, _, _, _ = self.places()
+        self.loading(d).wait()
+        for turn in (3, 2, 1, 0):
+            s = net.s ^ turn
+            if self.whole:
+                self.arrived(self.twin.at[s, d], s * self.count + d)
+                self.held[s, d] = self.held[s, d] + self.twin[s, d]
+            for part, device, slot, kind in {
+                3: ((0, net.y, 1, 1), (1, net.x, 1, 3)),
+                2: ((0, net.y, 0, 0),),
+                1: ((1, net.x, 0, 2),),
+                0: (),
+            }[turn]:
+                self.send(
+                    self.halves(self.held.at[s, d], part),
+                    self.first.at[part, slot, d],
+                    first + kind * self.count + d,
+                    device,
+                )
+
+    def add(self, block, other):
+        block[...] = block[...] + other[...]
+
+    def add_first(self, d):
+        net = self.net
+        _, first, second, _, _ = self.places()
+        for part, slot, kind, turn in ((0, 1, 1, 1), (1, 1, 3, 2), (0, 0, 0, 0), (1, 0, 2, 0)):
+            got = self.first.at[part, slot, d]
+            self.arrived(got, first + kind * self.count + d)
+            block = self.halves(self.held.at[net.s ^ turn, d], part)
+            self.add(block, got)
+            if turn:
+                device = net.x if part == 0 else net.y
+                self.send(block, self.second.at[part, d], second + part * self.count + d, device)
+
+    def add_second(self, d):
+        net = self.net
+        _, _, second, _, _ = self.places()
+        for part in range(2):
+            self.arrived(self.second.at[part, d], second + part * self.count + d)
+            self.add(self.halves(self.held.at[net.s, d], part), self.second.at[part, d])
+
+    def line_step(self, d):
+        net = self.net
+        _, _, _, right, left = self.places()
+        block = self.held.at[net.s, d]
+        if not self.whole:
+            self.out[d] = block[...].astype(self.out.dtype)
+            return
+
+        def from_left():
+            self.arrived(self.along.at[0, d], right + d)
+            self.add(block, self.along.at[0, d])
+
+        def from_right():
+            self.arrived(self.along.at[1, d], left + d)
+            self.add(block, self.along.at[1, d])
+
+        pl.when((net.z <= d) & (net.z > 0))(from_left)
+        pl.when((net.z >= d) & (net.z < net.line - 1))(from_right)
+        pl.when(net.z < d)(lambda: self.send(block, self.along.at[0, d], right + d, net.right))
+        pl.when(net.z > d)(lambda: self.send(block, self.along.at[1, d], left + d, net.left))
+
+        def keep():
+            self.out[...] = block[...].astype(self.out.dtype)
+
+        pl.when(net.z == d)(keep)
+
+    def finish(self):
+        net = self.net
+        _, first, second, right, left = self.places()
+        full = self.held.at[net.s, 0]
+        for d in range(self.count):
+            for s in range(4 if self.whole else 0):
+                self.sent(full, s * self.count + d)
+            for kind, part in enumerate((0, 0, 1, 1)):
+                self.sent(self.halves(full, part), first + kind * self.count + d)
+            for part in range(2):
+                self.sent(self.halves(full, part), second + part * self.count + d)
+            if self.whole:
+                pl.when(net.z < d)(lambda d=d: self.sent(full, right + d))
+                pl.when(net.z > d)(lambda d=d: self.sent(full, left + d))
+
+
+def ends_first(line):
+    return sorted(range(line), key=lambda d: min(d, line - 1 - d))
+
+
+def run_scatters(scatters):
+    lags = (("load", 0), ("add_core", 1), ("add_first", 2), ("add_second", 3), ("line_step", 4))
+    for wave in range(max(scatter.count for scatter in scatters) + lags[-1][1]):
+        for stage, lag in lags:
+            for scatter in scatters:
+                if 0 <= wave - lag < scatter.count:
+                    getattr(scatter, stage)(ends_first(scatter.count)[wave - lag])
+    for scatter in scatters:
+        scatter.finish()
+
+
+def scatter_scratch(count, rows, columns, halves, whole):
+    half = (rows // 2, columns) if halves is row_halves else (rows, columns // 2)
+    block = (rows, columns)
+    return [
+        pltpu.VMEM((4, count) + block, BF16),
+        pltpu.VMEM((4, count) + block if whole else (16, 128), BF16),
+        pltpu.VMEM((2, 2, count) + half, BF16),
+        pltpu.VMEM((2, count) + half, BF16),
+        pltpu.VMEM((2, count) + block if whole else (16, 128), BF16),
+        pltpu.SemaphoreType.DMA((12 * count,)),
+        pltpu.SemaphoreType.DMA((12 * count,)),
+        pltpu.SemaphoreType.DMA((count,)),
+    ]
+
+
+def scatter_kernel(line, plan, *refs):
+    count = len(plan)
+    sources, outs, scratch = refs[:count], refs[count : 2 * count], refs[2 * count :]
+    net = Net(line)
+    net.greet([net.x, net.y, net.core, net.left, net.right])
+    scatters = []
+    for i, (halves, whole) in enumerate(plan):
+        scatch = scratch[8 * i : 8 * i + 8]
+        scatters.append(Scatter(net, sources[i], outs[i], scatch[:5], scatch[5:], halves, whole))
+    run_scatters(scatters)
+
+
+def scatter_many(collective_id, name, sizes, arrays, plan):
+    square, line = sizes["seq"], sizes["mem"] // 2
+    blocks, outs, scratch = [], [], []
+    for array, (halves, whole) in zip(arrays, plan):
+        columns = array.shape[1]
+        if whole:
+            rows = array.shape[0] // (2 * square * line)
+            blocks.append(array.reshape(square, line, 2, rows, columns))
+            outs.append(jax.ShapeDtypeStruct((rows, columns), F32))
+            scratch += scatter_scratch(line, rows, columns, halves, True)
+        else:
+            rows = array.shape[0] // (square * PIECES)
+            blocks.append(array.reshape(square, PIECES, rows, columns))
+            outs.append(jax.ShapeDtypeStruct((PIECES, rows, columns), F32))
+            scratch += scatter_scratch(PIECES, rows, columns, halves, False)
+    moved = sum(a.size * a.dtype.itemsize for a in arrays)
+    sums = pl.pallas_call(
+        functools.partial(scatter_kernel, line, plan),
+        out_shape=outs,
+        in_specs=[pl.BlockSpec(memory_space=pl.ANY)] * len(plan),
+        out_specs=[pl.BlockSpec(memory_space=pltpu.VMEM)] * len(plan),
+        scratch_shapes=scratch,
+        compiler_params=params(collective_id=collective_id, has_side_effects=True),
+        cost_estimate=pl.CostEstimate(flops=0, bytes_accessed=2 * moved, transcendentals=0),
+        name=name,
+    )(*blocks)
+    return [s.reshape(-1, s.shape[-1]) for s in sums]
+
+
+def return_kernel(line, with_stats, *refs):
+    kinds = 2 if with_stats else 1
+    sources, outs = refs[:kinds], refs[kinds : 2 * kinds]
+    held, twin = refs[2 * kinds : 3 * kinds], refs[3 * kinds : 4 * kinds]
+    own, twin_sends, twin_recvs, sends, recvs = refs[4 * kinds :]
+    net = Net(line)
+    others = [(net.s, lax.rem(net.m + 2 * k, 2 * line)) for k in range(1, line)]
+    net.greet([net.core] + others)
+    places = [lax.rem(net.z + k, line) for k in (*range(1, line), 0)]
+    for d in places:
+        for i in range(kinds):
+            pltpu.make_async_copy(sources[i].at[d, net.c], held[i].at[d], own.at[i, d]).start()
+            remote(
+                sources[i].at[d, 1 - net.c], twin[i].at[d], twin_sends.at[i], twin_recvs.at[i], d, net.core
+            ).start()
+    for k, d in enumerate(places):
+        for i in range(kinds):
+            pltpu.make_async_copy(sources[i].at[d, net.c], held[i].at[d], own.at[i, d]).wait()
+            remote(
+                twin[i].at[d], twin[i].at[d], twin_sends.at[i], twin_recvs.at[i], d, net.core
+            ).wait_recv()
+        if with_stats:
+            mine, theirs = held[1][d], twin[1][d]
+            top = jnp.maximum(mine[:HEADS], theirs[:HEADS])
+            shares = [jnp.exp2(mine[:HEADS] - top), jnp.exp2(theirs[:HEADS] - top)]
+            held[1][d] = jnp.concatenate(
+                [top, mine[HEADS:] * shares[0] + theirs[HEADS:] * shares[1]], axis=0
+            )
+            shares = columns_of(jnp.concatenate(shares, axis=0))
+            for h in range(HEADS):
+                span = slice(h * 128, (h + 1) * 128)
+                held[0][d, :, span] = (
+                    held[0][d, :, span].astype(F32) * shares[:, h : h + 1]
+                    + twin[0][d, :, span].astype(F32) * shares[:, HEADS + h : HEADS + h + 1]
+                ).astype(BF16)
+        else:
+            held[0][d] = held[0][d] + twin[0][d]
+        for i in range(kinds):
+            if k < line - 1:
+                pltpu.make_async_remote_copy(
+                    src_ref=held[i].at[d],
+                    dst_ref=outs[i].at[net.z],
+                    send_sem=sends.at[i, k],
+                    recv_sem=recvs.at[i, net.z],
+                    device_id=(net.s, 2 * d + net.c),
+                    device_id_type=MESH,
+                ).start()
+            else:
+                pltpu.make_async_copy(held[i].at[d], outs[i].at[net.z], own.at[i, d]).start()
+    for i in range(kinds):
+        for k, d in enumerate(places):
+            remote(twin[i].at[d], twin[i].at[d], twin_sends.at[i], twin_recvs.at[i], d, net.core).wait_send()
+            if k < line - 1:
+                here = outs[i].at[d]
+                remote(here, here, sends.at[i], recvs.at[i], d, net.core).wait_recv()
+                pltpu.make_async_remote_copy(
+                    src_ref=held[i].at[d],
+                    dst_ref=here,
+                    send_sem=sends.at[i, k],
+                    recv_sem=recvs.at[i, d],
+                    device_id=net.core,
+                    device_id_type=MESH,
+                ).wait_send()
+            else:
+                pltpu.make_async_copy(held[i].at[d], outs[i].at[net.z], own.at[i, d]).wait()
+
+
+def return_home(collective_id, name, sizes, arrays):
+    line = sizes["mem"] // 2
+    blocks = [a.reshape((line, 2) + a.shape[1:]) for a in arrays]
+    kinds = len(arrays)
+    anywhere = pl.BlockSpec(memory_space=pl.ANY)
+    slots = [pltpu.VMEM((line,) + a.shape[1:], a.dtype) for a in arrays]
+    moved = sum(a.size * a.dtype.itemsize for a in arrays)
+    return pl.pallas_call(
+        functools.partial(return_kernel, line, kinds == 2),
+        out_shape=[jax.ShapeDtypeStruct((line,) + a.shape[1:], a.dtype) for a in arrays],
+        in_specs=[anywhere] * kinds,
+        out_specs=[anywhere] * kinds,
+        scratch_shapes=slots
+        + slots
+        + [pltpu.SemaphoreType.DMA((kinds, line))] * 5,
+        compiler_params=params(collective_id=collective_id, has_side_effects=True),
+        cost_estimate=pl.CostEstimate(flops=0, bytes_accessed=2 * moved, transcendentals=0),
+        name=name,
+    )(*blocks)
 
 
 def mask_kernel(blocks, order_ref, base_ref, index_ref, bits_ref):
@@ -209,7 +729,9 @@
     return jnp.where(lax.broadcasted_iota(jnp.int32, (rows, keys), 1) <= row, 0.0, FLOOR)
 
 
-def local_forward_kernel(scale, place_ref, q_ref, k_ref, v_ref, o_ref, st_ref):
+def local_forward_kernel(scale, place_ref, q_ref, kv_ref, o_ref, st_ref):
+    width = q_ref.shape[1]
+    k_ref, v_ref = kv_ref.at[:, :width], kv_ref.at[:, width:]
     bias = causal_bias(place_ref, q_ref.shape[0], k_ref.shape[0])
     maxima, sums = [], []
     for h in range(HEADS):
@@ -227,15 +749,15 @@
     return pl.BlockSpec(shape, lambda *_: (0,) * len(shape))
 
 
-def local_forward(place, queries, keys, values, scale):
+def local_forward(place, queries, kv, scale):
     rows, width = queries.shape
-    length = keys.shape[0]
+    length = kv.shape[0]
     return pl.pallas_call(
         functools.partial(local_forward_kernel, scale),
         grid_spec=pltpu.PrefetchScalarGridSpec(
             num_scalar_prefetch=1,
             grid=(1,),
-            in_specs=[whole(rows, width), whole(length, width), whole(length, width)],
+            in_specs=[whole(rows, width), whole(length, 2 * width)],
             out_specs=[whole(rows, width), whole(STATS, rows)],
         ),
         out_shape=[
@@ -244,12 +766,15 @@
         ],
         compiler_params=params(),
         name="local_forward",
-    )(place, queries, keys, values)
+    )(place, queries, kv)
 
 
 def local_backward_kernel(
-    scale, place_ref, q_ref, g_ref, st_ref, k_ref, v_ref, dq_ref, dk_ref, dv_ref
+    scale, place_ref, q_ref, g_ref, st_ref, kv_ref, dq_ref, dkv_ref
 ):
+    width = q_ref.shape[1]
+    k_ref, v_ref = kv_ref.at[:, :width], kv_ref.at[:, width:]
+    dk_ref, dv_ref = dkv_ref.at[:, :width], dkv_ref.at[:, width:]
     bias = causal_bias(place_ref, q_ref.shape[0], k_ref.shape[0])
     stats = columns_of(st_ref[...])
     for h in range(HEADS):
@@ -264,9 +789,9 @@
         dv_ref[:, span] = dot(weights.astype(BF16), grad, TN).astype(BF16)
 
 
-def local_backward(place, queries, grads, stats, keys, values, scale):
+def local_backward(place, queries, grads, stats, kv, scale):
     rows, width = queries.shape
-    length = keys.shape[0]
+    length = kv.shape[0]
     return pl.pallas_call(
         functools.partial(local_backward_kernel, scale),
         grid_spec=pltpu.PrefetchScalarGridSpec(
@@ -276,22 +801,43 @@
                 whole(rows, width),
                 whole(rows, width),
                 whole(STATS, rows),
-                whole(length, width),
-                whole(length, width),
+                whole(length, 2 * width),
             ],
-            out_specs=[whole(rows, width), whole(length, width), whole(length, width)],
+            out_specs=[whole(rows, width), whole(length, 2 * width)],
         ),
         out_shape=[
             jax.ShapeDtypeStruct((rows, width), F32),
-            jax.ShapeDtypeStruct((length, width), BF16),
-            jax.ShapeDtypeStruct((length, width), BF16),
+            jax.ShapeDtypeStruct((length, 2 * width), BF16),
         ],
         compiler_params=params(),
         name="local_backward",
-    )(place, queries, grads, stats, keys, values)
+    )(place, queries, grads, stats, kv)
+
+
+REACH = {"all": ("seq", "mem"), "line": "mem", "square": "seq"}
+
+
+def gather_plain(collective_id, name, sizes, arrays, plan):
+    return [lax.all_gather(a, REACH[reach], axis=0) for a, (_, reach) in zip(arrays, plan)]
+
+
+def scatter_plain(collective_id, name, sizes, arrays, plan):
+    return [
+        lax.psum_scatter(
+            a, REACH["all"] if whole else REACH["square"], scatter_dimension=0, tiled=True
+        ).astype(F32)
+        for a, (_, whole) in zip(arrays, plan)
+    ]
+
+
+def return_plain(collective_id, name, sizes, arrays):
+    return [
+        lax.all_to_all(a, "mem", split_axis=0, concat_axis=0, tiled=True) for a in arrays
+    ]
 
 
 def per_device(
+    sizes,
     tokens,
     cached_keys,
     cached_values,
@@ -308,9 +854,12 @@
     gain_ffn,
     cotangent,
 ):
-    both = ("seq", "mem")
-    gather = functools.partial(lax.all_gather, axis=0, tiled=True)
-    scatter = functools.partial(lax.psum_scatter, scatter_dimension=0, tiled=True)
+    near = sizes["seq"] == 4 and sizes["mem"] % 2 == 0 and 4 <= sizes["mem"] <= 16
+    gather, scatter, send_home = (
+        (gather_many, scatter_many, return_home)
+        if near
+        else (gather_plain, scatter_plain, return_plain)
+    )
     inputs = tokens[0].astype(F32)
     rows, width = inputs.shape
     hidden_width = w_gate.shape[1]
@@ -322,9 +871,16 @@
 
     gains = jnp.zeros((w_query.shape[0], 128), BF16)
     gains = gains.at[:, 0].set(gain_attn).at[:, 1].set(gain_ffn)
-    first_weights = gather(jnp.concatenate([w_query, w_key, w_value, gains], axis=1), both)
+    first_shard = jnp.concatenate([w_query, w_key, w_value, gains], axis=1)
     flag_rows = jnp.broadcast_to(has_memory[:, None], (8, 128))
-    shared = gather(jnp.concatenate([knn_index[0], flag_rows], axis=0)[None], "mem")
+    first_weights, shared = gather(
+        1,
+        "gather_first",
+        sizes,
+        [first_shard, jnp.concatenate([knn_index[0], flag_rows], axis=0)],
+        [(row_halves, "all"), (row_halves, "line")],
+    )
+    first_weights = first_weights.reshape(-1, first_shard.shape[1])
     all_index, flags = shared[:, :rows], shared[:, rows, 0]
     segments = flags.shape[0]
     order = jnp.argsort(jnp.where(flags > 0, 0, 1), stable=True)[: segments // 2].astype(jnp.int32)
@@ -333,12 +889,6 @@
     qkv_weight = first_weights[:, : 3 * width]
     gain_first = first_weights[:, 3 * width].astype(F32)
     gain_second = first_weights[:, 3 * width + 1].astype(F32)
-    out_gate_up = gather(jnp.concatenate([w_out, w_gate, w_up], axis=1), both)
-    down_weight = gather(w_down, both)
-    out_weight = out_gate_up[:, :width]
-    gate_weight = out_gate_up[:, width : width + hidden_width]
-    up_weight = out_gate_up[:, width + hidden_width :]
-
     positions = lax.axis_index("seq") * rows + jnp.arange(rows)
     cosine, sine = angles_for(positions, head_width)
     normed_one, norm_one_back = jax.vjp(rms_norm, inputs, gain_first)
@@ -346,18 +896,27 @@
     qkv = dot(norm_one, qkv_weight)
     queries = rotate(qkv[:, :width], cosine, sine).astype(BF16)
     keys = rotate(qkv[:, width : 2 * width], cosine, sine).astype(BF16)
-    values = qkv[:, 2 * width :].astype(BF16)
-    all_queries = gather(queries[None], "mem")
-    segment_keys, segment_values = gather(keys, "seq"), gather(values, "seq")
+    keys_values = jnp.concatenate([keys, qkv[:, 2 * width :].astype(BF16)], axis=1)
+    out_shard = jnp.concatenate([w_out, w_gate, w_up], axis=1)
+    all_queries, segment_kv, out_gate_up, down_weight = gather(
+        2,
+        "gather_second",
+        sizes,
+        [queries, keys_values, out_shard, w_down],
+        [(row_halves, "line"), (row_halves, "square"), (row_halves, "all"), (column_halves, "all")],
+    )
+    segment_kv = segment_kv.reshape(-1, 2 * width)
+    down_weight = down_weight.reshape(-1, width)
+    out_gate_up = out_gate_up.reshape(width, -1)
+    out_weight = out_gate_up[:, :width]
+    gate_weight = out_gate_up[:, width : width + hidden_width]
+    up_weight = out_gate_up[:, width + hidden_width :]
 
     owner_out, owner_stats = owner_forward(
         order, all_queries, bits, cached_keys, cached_values, scale
     )
-    local_out, local_stats = local_forward(place, queries, segment_keys, segment_values, scale)
-    exchange = functools.partial(
-        lax.all_to_all, axis_name="mem", split_axis=0, concat_axis=0, tiled=True
-    )
-    peer_out, peer_stats = exchange(owner_out), exchange(owner_stats)
+    local_out, local_stats = local_forward(place, queries, segment_kv, scale)
+    peer_out, peer_stats = send_home(3, "return_outputs", sizes, [owner_out, owner_stats])
     live = has_memory[0] > 0
     peer_max = jnp.where(live, peer_stats[:, :HEADS], LOW)
     peer_sum = jnp.where(live, peer_stats[:, HEADS:], 0.0)
@@ -399,7 +958,13 @@
         (grad_attention.astype(F32) * attention).reshape(rows, HEADS, head_width), axis=2
     ).T
     back_stats = jnp.concatenate([log_total, grad_dots], axis=0)
-    all_grads, all_stats = gather(grad_attention[None], "mem"), gather(back_stats[None], "mem")
+    all_grads, all_stats = gather(
+        4,
+        "gather_grads",
+        sizes,
+        [grad_attention, back_stats],
+        [(row_halves, "line"), (row_halves, "line")],
+    )
 
     early = jnp.concatenate(
         [
@@ -409,19 +974,24 @@
         ],
         axis=1,
     ).astype(BF16)
-    early_sum = scatter(early, both)
-    down_sum = scatter(dot(hidden, grad_out, TN).astype(BF16), both)
-
-    local_dq, local_dk, local_dv = local_backward(
-        place, queries, grad_attention, back_stats, segment_keys, segment_values, scale
+    early_sum, down_sum = scatter(
+        5,
+        "scatter_early",
+        sizes,
+        [early, dot(hidden, grad_out, TN).astype(BF16)],
+        [(row_halves, True), (column_halves, True)],
+    )
+
+    local_dq, local_dkv = local_backward(
+        place, queries, grad_attention, back_stats, segment_kv, scale
     )
     owner_grads = owner_backward(
         order, all_queries, all_grads, all_stats, bits, cached_keys, cached_values, scale
     )
-    peer_grads = exchange(owner_grads)
+    (peer_grads,) = send_home(6, "return_grads", sizes, [owner_grads])
     grad_queries = local_dq + jnp.sum(jnp.where(live, peer_grads.astype(F32), 0.0), axis=0)
-    grad_keys_mine = scatter(local_dk, "seq").astype(F32)
-    grad_value_in = scatter(local_dv, "seq")
+    (grad_kv,) = scatter(7, "scatter_keys", sizes, [local_dkv], [(row_halves, False)])
+    grad_keys_mine, grad_value_in = grad_kv[:, :width], grad_kv[:, width:].astype(BF16)
     grad_query_in = rotate(grad_queries, cosine, -sine).astype(BF16)
     grad_key_in = rotate(grad_keys_mine, cosine, -sine).astype(BF16)
     grad_in = jnp.concatenate([grad_query_in, grad_key_in, grad_value_in], axis=1)
@@ -439,8 +1009,7 @@
         ],
         axis=1,
     )
-    late_sum = scatter(late, both).astype(F32)
-    early_sum = early_sum.astype(F32)
+    (late_sum,) = scatter(8, "scatter_late", sizes, [late], [(row_halves, True)])
     return (
         mixed[None],
         grad_inputs[None],
@@ -451,7 +1020,7 @@
         late_sum[:, 3 * width],
         early_sum[:, width : width + hidden_width],
         early_sum[:, width + hidden_width :],
-        down_sum.astype(F32),
+        down_sum,
         late_sum[:, 3 * width + 1],
     )
 
@@ -460,7 +1029,7 @@
     rows, owned, feature = P("mem", "seq", None), P(None, "mem", None), P(("seq", "mem"), None)
     gain = P(("seq", "mem"))
     return jax.shard_map(
-        per_device,
+        functools.partial(per_device, dict(mesh.shape)),
         mesh=mesh,
         in_specs=(
             (rows, owned, owned, rows, P("mem"))

time: 1080 us -> 820 us (0.76)
  the two profiles are of different devices: /device:TPU:0 before, /device:TPU:23 now
where the time goes in v2:
time: 820 us; the launch traced here: 811 us
  Pallas kernels  688 us (84%)
  matrix products  47.3 us (6%)
  other arithmetic  40.2 us (5%)
  local copies, waits for them, and re-layouts  32.8 us (4%)
    pallas_call x3, Pallas kernels, scatter_many(): pl.pallas_call(functools.partial(scatter_kernel, line, plan), out_shape=o...  283 us
    pallas_call x3, Pallas kernels, gather_many(): pl.pallas_call(functools.partial(gather_kernel, line, plan), out_shape=[j...  195 us
    pallas_call x2, Pallas kernels, return_home(): pl.pallas_call(functools.partial(return_kernel, line, kinds == 2), out_sh...  108 us
    dot_general x15, matrix products, dot(): return lax.dot_general(left, right, dims, preferred_element_type=F32)  47.3 us
    pallas_call x1, Pallas kernels, mask_bits(): pl.pallas_call(functools.partial(mask_kernel, mem_dev // 128), grid_spec=...  41.1 us
    pallas_call x1, Pallas kernels, owner_backward(): pl.pallas_call(functools.partial(owner_backward_kernel, scale), grid_spec...  21 us
    pallas_call x1, Pallas kernels, owner_forward(): pl.pallas_call(functools.partial(owner_forward_kernel, scale), grid_spec=...  20.7 us

profile of v2, /device:TPU:23, one launch (start us, length us, event | category | flops | bytes accessed | tf_op | source)
XLA Modules:
  0.0 811.3 jit_solution(12670564734679568924)
XLA Ops:
  8.7 34.0 %gather_first.1 = (bf16[32,32,3200]{2,1,0:T(8,128)(2,1)}, s32[8,264,128]{2,1,0:T(8,128)}) custom-call(bf16[32,3200]{1,0:T(8,128)(2,1)} %pad_maximum_fusion.11.refs_0_, s32[264,128]{1,0:T(8,128)} %concatenate.57.refs_1_), custom_call_target="tpu_custom_call" | custom-call | bytes 15269888 | tf_op jit(solution)/shard_map/gather_first/pallas_call | solution.py:302
  45.4 4.8 fusion.2
  58.1 123.7 %gather_second.1 = (bf16[8,256,1024]{2,1,0:T(8,128)(2,1)}, bf16[4,256,2048]{2,1,0:T(8,128)(2,1)}, bf16[32,32,6656]{2,1,0:T(8,128)(2,1)}, bf16[32,88,1024]{2,1,0:T(8,128)(2,1)}) custom-call(bf16[256,1024]{1,0:T(8,128)(2,1)} %bitcast.115, bf16[256,2048]{1,0:T(8,128)(2,1)} %pad_maximum_fusion.3.refs_1_, bf16[32,6656]{1,0:T(8,128)(2,1)} %pad_maximum_fusion.10.refs_2_, ...), custom_call_target="tpu_custom_call" | custom-call | bytes 55574528 | tf_op jit(solution)/shard_map/gather_second/pallas_call | solution.py:302
  184.2 41.1 %mask_bits.1.bits_ref = s32[4,256,128]{2,1,0:T(8,128)} custom-call(s32[4]{0:T(128)} %bitcast.149, s32[1]{0:T(128)} %bitcast.10.base_ref, s32[8,256,128]{2,1,0:T(8,128)} %slice.174.index_ref), custom_call_target="tpu_custom_call" | custom-call | tf_op jit(solution)/shard_map/mask_bits/pallas_call | solution.py:617
  225.3 20.7 %owner_forward.1 = (bf16[8,256,1024]{2,1,0:T(8,128)(2,1)}, f32[8,16,256]{2,1,0:T(8,128)}) custom-call(s32[4]{0:T(128)} %bitcast.150, bf16[8,256,1024]{2,1,0:T(8,128)(2,1)} %get-tuple-element.84.q_ref, s32[4,256,128]{2,1,0:T(8,128)} %mask_bits.1.bits_ref, bf16[8,1024,1024]{2,1,0:T(8,128)(2,1)} %k_ref.3, bf16[8,1024,1024]{2,1,0:T(8,128)(2,1)} %v_ref.3), custom_call_target="tpu_custom_call" | custom-call | tf_op jit(solution)/shard_map/owner_forward/pallas_call | solution.py:657
  246.0 52.6 %return_outputs.1 = (bf16[4,256,1024]{2,1,0:T(8,128)(2,1)}, f32[4,16,256]{2,1,0:T(8,128)}) custom-call(bf16[4,2,256,1024]{3,2,1,0:T(8,128)(2,1)} %bitcast.122, f32[4,2,16,256]{3,2,1,0:T(8,128)} %bitcast.134), custom_call_target="tpu_custom_call" | custom-call | bytes 8650752 | tf_op jit(solution)/shard_map/return_outputs/pallas_call | solution.py:578
  299.4 7.6 local_forward.1
  308.7 2.6 broadcast_in_dim.80
  311.3 5.3 reshape.369
  316.6 3.7 multiply_reduce_fusion
  322.6 2.5 multiply_reduce_fusion.3
  325.1 6.3 convolution_bitcast_fusion
  331.8 6.0 fusion.6
  337.8 6.4 fusion.14
  344.3 2.7 fusion.25
  348.7 2.4 multiply_reduce_fusion.1
  357.2 10.8 %local_backward.1 = (f32[256,1024]{1,0:T(8,128)}, bf16[1024,2048]{1,0:T(8,128)(2,1)}) custom-call(s32[1]{0:T(128)} %bitcast.1.place_ref, bf16[256,1024]{1,0:T(8,128)(2,1)} %bitcast.117, bf16[256,1024]{1,0:T(8,128)(2,1)} %copy-done.1, f32[16,256]{1,0:T(8,128)} %pad_maximum_fusion.12.st_ref.refs_1_, bf16[1024,2048]{1,0:T(8,128)(2,1)} %bitcast.110), custom_call_target="tpu_custom_call" | custom-call | tf_op jit(solution)/shard_map/local_backward/pallas_call | solution.py:795
  368.0 40.4 %scatter_keys.1 = f32[4,64,2048]{2,1,0:T(8,128)} custom-call(bf16[4,4,64,2048]{3,2,1,0:T(8,128)(2,1)} %bitcast.121), custom_call_target="tpu_custom_call" | custom-call | bytes 8388608 | tf_op jit(solution)/shard_map/scatter_keys/pallas_call | solution.py:491
  409.7 37.7 %gather_grads.1 = (bf16[8,256,1024]{2,1,0:T(8,128)(2,1)}, f32[8,16,256]{2,1,0:T(8,128)}) custom-call(bf16[256,1024]{1,0:T(8,128)(2,1)} %copy-done.1, f32[16,256]{1,0:T(8,128)} %pad_maximum_fusion.12.st_ref.refs_1_), custom_call_target="tpu_custom_call" | custom-call | bytes 8650752 | tf_op jit(solution)/shard_map/gather_grads/pallas_call | solution.py:302
  447.4 21.0 %owner_backward.1 = bf16[8,256,1024]{2,1,0:T(8,128)(2,1)} custom-call(s32[4]{0:T(128)} %bitcast.151, bf16[8,256,1024]{2,1,0:T(8,128)(2,1)} %get-tuple-element.84.q_ref, bf16[8,256,1024]{2,1,0:T(8,128)(2,1)} %get-tuple-element.92.g_ref, f32[8,16,256]{2,1,0:T(8,128)} %get-tuple-element.93.st_ref, s32[4,256,128]{2,1,0:T(8,128)} %mask_bits.1.bits_ref, ...), custom_call_target="tpu_custom_call" | custom-call | tf_op jit(solution)/shard_map/owner_backward/pallas_call | solution.py:705
  468.4 55.7 %return_grads.1 = bf16[4,256,1024]{2,1,0:T(8,128)(2,1)} custom-call(bf16[4,2,256,1024]{3,2,1,0:T(8,128)(2,1)} %bitcast.108), custom_call_target="tpu_custom_call" | custom-call | bytes 8388608 | tf_op jit(solution)/shard_map/return_grads/pallas_call | solution.py:578
  524.2 2.3 select_reduce_fusion
  530.5 2.0 fusion.32
  536.3 2.0 scatter.19
  538.3 3.3 convolution_convert_fusion.3
  541.6 3.2 pad_maximum_fusion.1
  544.8 68.0 %scatter_late.1 = f32[32,3200]{1,0:T(8,128)} custom-call(bf16[4,4,2,32,3200]{4,3,2,1,0:T(8,128)(2,1)} %bitcast.107), custom_call_target="tpu_custom_call" | custom-call | bytes 13107200 | tf_op jit(solution)/shard_map/scatter_late/pallas_call | solution.py:491
  612.8 1.8 fusion.57
  618.9 6.0 pad_maximum_fusion.refs_0_
  624.9 4.1 convolution_convert_fusion
  629.0 175.0 %scatter_early.1 = (f32[32,6656]{1,0:T(8,128)}, f32[88,1024]{1,0:T(8,128)}) custom-call(bf16[4,4,2,32,6656]{4,3,2,1,0:T(8,128)(2,1)} %pad_maximum_fusion.refs_0_, bf16[4,4,2,88,1024]{4,3,2,1,0:T(8,128)(2,1)} %bitcast.104), custom_call_target="tpu_custom_call" | custom-call | bytes 38797312 | tf_op jit(solution)/shard_map/scatter_early/pallas_call | solution.py:491
  807.1 2.0 fusion.56
  (159 shorter events, 50.9 us)
Async XLA Ops:
  44.1 6.1 copy-start.24
  45.3 4.9 copy-start.26
  45.3 4.9 copy-start.28
  53.4 4.0 copy-start.20
  53.4 4.0 copy-start.21
  53.4 4.0 copy-start.23
  54.0 127.9 %copy-start.15 = (s32[8,264,128]{2,1,0:T(8,128)S(1)}, s32[8,264,128]{2,1,0:T(8,128)}, u32[]{:S(2)}) copy-start(s32[8,264,128]{2,1,0:T(8,128)} %get-tuple-element.82) | copy-start | bytes 3244036
  298.6 9.1 %copy-start.19 = (f32[4,16,256]{2,1,0:T(8,128)S(1)}, f32[4,16,256]{2,1,0:T(8,128)}, u32[]{:S(2)}) copy-start(f32[4,16,256]{2,1,0:T(8,128)} %get-tuple-element.87) | copy-start | bytes 196612
  316.6 3.7 copy-start.22
  320.8 4.2 copy-start.7
  325.0 23.6 %copy-start.2 = (f32[256,1024]{1,0:T(8,128)}, f32[256,1024]{1,0:T(8,128)S(1)}, u32[]{:S(2)}) copy-start(f32[256,1024]{1,0:T(8,128)S(1)} %get-tuple-element.133) | copy-start | bytes 3145732
  331.8 6.0 copy-start.31
  331.8 12.4 %slice-start.6 = ((s8[5767168]{0:T(1024)(128)(4,1)}), s8[4194304]{0:T(1024)(128)(4,1)S(1)}, s32[]{:S(2)}) async-start(s8[5767168]{0:T(1024)(128)(4,1)} %bitcast.161), calls=%async_computation.6 | async-start | bytes 8388608
  337.8 6.4 slice-start.7
  337.8 9.1 %slice-start.2 = ((s8[13631488]{0:T(1024)(128)(4,1)}), s8[4194304]{0:T(1024)(128)(4,1)S(1)}, s32[]{:S(2)}) async-start(s8[13631488]{0:T(1024)(128)(4,1)} %bitcast.155), calls=%async_computation.2 | async-start | bytes 8388608
  337.8 9.1 %slice-start.3 = ((s8[13631488]{0:T(1024)(128)(4,1)}), s8[4194304]{0:T(1024)(128)(4,1)S(1)}, s32[]{:S(2)}) async-start(s8[13631488]{0:T(1024)(128)(4,1)} %bitcast.155), calls=%async_computation.3 | async-start | bytes 8388608
  337.8 9.1 %slice-start.4 = ((s8[13631488]{0:T(1024)(128)(4,1)}), s8[4194304]{0:T(1024)(128)(4,1)S(1)}, s32[]{:S(2)}) async-start(s8[13631488]{0:T(1024)(128)(4,1)} %bitcast.155), calls=%async_computation.4 | async-start | bytes 8388608
  344.2 2.7 copy-start.3
  344.2 2.7 copy-start.12
  344.2 4.5 copy-start.10
  344.2 2.7 slice-start.5
  353.6 3.6 copy-start.1
  409.7 119.2 %copy-start.16 = (bf16[256,1024]{1,0:T(8,128)(2,1)}, bf16[256,1024]{1,0:T(8,128)(2,1)S(1)}, u32[]{:S(2)}) copy-start(bf16[256,1024]{1,0:T(8,128)(2,1)S(1)} %slice.282) | copy-start | bytes 1572868
  468.4 58.1 %copy-start.14 = (f32[256,1024]{1,0:T(8,128)S(1)}, f32[256,1024]{1,0:T(8,128)}, u32[]{:S(2)}) copy-start(f32[256,1024]{1,0:T(8,128)} %get-tuple-element.91) | copy-start | bytes 3145732
  524.2 2.7 copy-start
  527.2 3.1 slice-start.1
  528.0 2.5 copy-start.6
  528.4 4.1 copy-start.17
  528.8 3.7 copy-start.18
  544.8 69.8 %copy-start.13 = (bf16[256,2816]{1,0:T(8,128)(2,1)S(1)}, bf16[256,2816]{1,0:T(8,128)(2,1)}, u32[]{:S(2)}) copy-start(bf16[256,2816]{1,0:T(8,128)(2,1)} %copy-done.12) | copy-start | bytes 4325380
  618.8 6.0 copy-start.4
  618.9 6.0 copy-start.9
  (8 other events, 17.3 us)

commit v3 on v1

v3 whole, which is shorter than its diff:
```python
import functools

import jax
import jax.numpy as jnp
from jax import lax
from jax.experimental import pallas as pl
from jax.experimental.pallas import tpu as pltpu
from jax.sharding import PartitionSpec as P

HEADS = 8
EPSILON = 1e-05
FLOOR = -1e30
LOW = -1e29
LOG2E = 1.4426950408889634
STATS = 16
PIECES = 4
ORDERS = {
    ("first", 4): (
        7, 0, 7, 8, 9, 1, 7, 8, 2, 10, 10, 3, 9, 11, 11, 12, 4, 10, 13, 12, 8, 13, 9, 11, 6, 5,
        13, 12,
    ),
    ("second", 4): (
        28, 29, 21, 36, 14, 36, 30, 7, 22, 0, 36, 23, 32, 31, 16, 15, 2, 9, 36, 34, 36, 1, 25, 36,
        17, 30, 33, 32, 8, 34, 4, 28, 36, 11, 27, 35, 3, 33, 36, 18, 29, 30, 35, 24, 19, 13, 34,
        26, 31, 12, 20, 33, 5, 32, 10, 6, 28, 29, 35, 31,
    ),
    ("third", 4): (
        4, 18, 6, 5, 18, 11, 1, 8, 6, 7, 25, 13, 12, 2, 25, 4, 3, 1, 25, 25, 10, 0, 10, 15, 10,
        19, 14, 0, 17, 20, 25, 7, 22, 25, 3, 14, 11, 12, 2, 16, 22, 8, 20, 7, 18, 16, 6, 21, 19,
        24, 4, 21, 17, 11, 13, 25, 15, 19, 17, 5, 22, 25, 24, 21, 9, 9, 13, 20, 12, 8, 5, 23, 9,
        23, 15, 24, 14, 16, 23,
    ),
    ("fourth", 4): (
        0, 7, 14, 21, 28, 35, 35, 1, 35, 2, 35, 8, 35, 9, 35, 15, 16, 35, 35, 22, 23, 29, 30, 3,
        4, 10, 11, 17, 18, 24, 25, 31, 32, 5, 6, 12, 13, 19, 20, 26, 27, 33, 34,
    ),
    ("fifth", 4): (
        4, 4, 2, 12, 8, 16, 8, 4, 12, 20, 20, 5, 0, 0, 8, 13, 21, 16, 13, 17, 20, 8, 16, 9, 5, 9,
        6, 10, 8, 12, 11, 4, 13, 10, 2, 9, 16, 1, 1, 21, 5, 14, 17, 18, 9, 12, 10, 4, 6, 5, 19,
        22, 21, 20, 13, 17, 22, 17, 16, 15, 3, 20, 10, 13, 19, 6, 22, 14, 19, 12, 5, 3, 14, 18,
        21, 15, 11, 23, 14, 9, 18, 10, 11, 17, 7, 15, 22, 7, 14, 15, 18, 21, 7, 6, 22, 11, 18, 23,
        15, 6, 7, 19, 23, 19, 7, 23, 23, 11,
    ),
    ("sixth", 4): (
        0, 0, 3, 2, 1, 0, 1, 0, 0, 1, 2, 1, 1, 2, 3, 2, 2, 3, 3, 3,
    ),
}
F32 = jnp.float32
BF16 = jnp.bfloat16
VMEM_LIMIT = 56 * 1024 * 1024
NT = (((1,), (1,)), ((), ()))
TN = (((0,), (0,)), ((), ()))


def dot(left, right, dims=(((1,), (0,)), ((), ()))):
    return lax.dot_general(left, right, dims, preferred_element_type=F32)


def angles_for(positions, head_width):
    exponent = jnp.arange(head_width // 2, dtype=F32) * (2.0 / head_width)
    frequency = jnp.power(10000.0, -exponent)
    turned = positions.astype(F32)[:, None] * frequency[None, :]
    return (jnp.cos(turned), jnp.sin(turned))


def params(**more):
    return pltpu.CompilerParams(vmem_limit_bytes=VMEM_LIMIT, **more)


def spread(columns, width=128):
    lanes = lax.broadcasted_iota(jnp.int32, (columns[0].shape[0], width), 1)
    result = jnp.zeros((columns[0].shape[0], width), F32)
    for place, column in enumerate(columns):
        result = jnp.where(lanes == place, column, result)
    return result


def columns_of(rows_by_stat):
    count, width = rows_by_stat.shape
    padded = jnp.concatenate([rows_by_stat, jnp.zeros((128 - count, width), F32)], axis=0)
    return padded.T


MESH = pl.DeviceIdType.MESH


class Net:
    def __init__(self, line):
        self.line = line
        self.s, self.m = lax.axis_index("seq"), lax.axis_index("mem")
        self.c, self.z = self.m % 2, self.m // 2
        self.x, self.y, self.core = (self.s ^ 1, self.m), (self.s ^ 2, self.m), (self.s, self.m ^ 1)
        self.right = (self.s, (self.m + 2) % (2 * line))
        self.left = (self.s, (self.m + 2 * line - 2) % (2 * line))

    def others(self):
        ring = 2 * self.line
        return [(self.s, lax.rem(self.m + 2 * k, ring)) for k in range(1, self.line)]

    def greet(self, others):
        barrier = pltpu.get_barrier_semaphore()
        for other in others:
            pl.semaphore_signal(barrier, inc=1, device_id=other, device_id_type=MESH)
        pl.semaphore_wait(barrier, len(others))


def remote(src, dst, sends, recvs, place, device):
    return pltpu.make_async_remote_copy(
        src_ref=src,
        dst_ref=dst,
        send_sem=sends.at[place],
        recv_sem=recvs.at[place],
        device_id=device,
        device_id_type=MESH,
    )


def row_halves(ref, part):
    half = ref.shape[-2] // 2
    return ref.at[pl.ds(part * half, half)]


def column_halves(ref, part):
    half = ref.shape[-1] // 2
    return ref.at[:, pl.ds(part * half, half)]


class Gather:
    def __init__(self, net, src, out, sends, recvs, own, index, halves, line=True, square=True, core=True):
        self.net, self.src, self.out, self.sends, self.recvs, self.own = net, src, out, sends, recvs, own
        self.index, self.halves = index, halves
        self.line, self.square, self.core = line, square, core

    def slot(self, s, z):
        return self.out.at[self.index(s, z, self.net.c)]

    def send(self, block, target, place, device):
        copy = remote(block, target, self.sends, self.recvs, place, device)
        copy.start()

    def sent(self, block, place):
        remote(block, block, self.sends, self.recvs, place, self.net.core).wait_send()

    def arrived(self, block, place):
        remote(block, block, self.sends, self.recvs, place, self.net.core).wait_recv()

    def places(self):
        z = self.net.line
        right, left, square, core = 0, z, 2 * z, 8 * z
        return right, left, square, core

    def chain(self, k, from_left):
        net = self.net
        z = net.z - k if from_left else net.z + k
        present = z >= 0 if from_left else z < net.line
        for stage in (self.have, self.pass_square, self.end_square) if self.square else (self.have,):
            if k == 0:
                stage(0, net.z, None)
            else:
                pl.when(present)(lambda stage=stage: stage(k, z, from_left))
            yield

    def chains(self):
        chains = [self.chain(0, True)]
        for k in range(1, self.net.line if self.line else 1):
            chains += [self.chain(k, True), self.chain(k, False)]
        return chains

    def have(self, k, z, from_left):
        net = self.net
        right, left, square, core = self.places()
        target = self.slot(net.s, z)
        block = self.src if k == 0 else target
        if k == 0:
            pltpu.make_async_copy(self.src, target, self.own).start()
        else:
            self.arrived(target, (right if from_left else left) + z)
        if self.line:
            if from_left is not False:
                pl.when(net.z < net.line - 1)(lambda: self.send(block, target, right + z, net.right))
            if from_left is not True:
                pl.when(net.z > 0)(lambda: self.send(block, target, left + z, net.left))
        if self.square:
            for kind, part, device in ((0, 0, net.x), (2, 1, net.y), (1, 0, net.y), (3, 1, net.x)):
                self.send(
                    self.halves(block, part),
                    self.halves(target, part),
                    square + kind * net.line + z,
                    device,
                )
        if self.core:
            self.send(block, target, core + z, net.core)

    def pass_square(self, k, z, from_left):
        net = self.net
        _, _, square, core = self.places()
        for kind, part, other, then, device, mirror in (
            (0, 0, net.s ^ 1, 4, net.y, 1),
            (2, 1, net.s ^ 2, 5, net.x, 2),
        ):
            block = self.halves(self.slot(other, z), part)
            self.arrived(block, square + kind * net.line + z)
            self.send(block, block, square + then * net.line + z, device)
            if self.core:
                self.send(block, block, core + mirror * net.line + z, net.core)

    def end_square(self, k, z, from_left):
        net = self.net
        _, _, square, core = self.places()
        for kind, part, other, mirror in self.last(net):
            block = self.halves(self.slot(other, z), part)
            self.arrived(block, square + kind * net.line + z)
            if self.core:
                self.send(block, block, core + mirror * net.line + z, net.core)

    def last(self, net):
        return (
            (1, 0, net.s ^ 2, 3),
            (3, 1, net.s ^ 1, 5),
            (4, 0, net.s ^ 3, 4),
            (5, 1, net.s ^ 3, 6),
        )

    def finish(self):
        net = self.net
        right, left, square, core = self.places()
        own = self.slot(net.s, net.z)
        pltpu.make_async_copy(self.src, own, self.own).wait()
        if self.core:
            for z in range(net.line if self.line else 1):
                z = z if self.line else net.z
                for mirror, part, other in (
                    (0, None, net.s),
                    (1, 0, net.s ^ 1),
                    (2, 1, net.s ^ 2),
                    (3, 0, net.s ^ 2),
                    (4, 0, net.s ^ 3),
                    (5, 1, net.s ^ 1),
                    (6, 1, net.s ^ 3),
                ):
                    if part is not None and not self.square:
                        continue
                    block = self.out.at[self.index(other, z, 1 - net.c)]
                    block = block if part is None else self.halves(block, part)
                    self.arrived(block, core + mirror * net.line + z)
                    self.sent(block, core + mirror * net.line + z)
        if self.square:
            half = [self.halves(own, 0), self.halves(own, 1)]
            for z in range(net.line if self.line else 1):
                z = z if self.line else net.z
                for kind, part in ((0, 0), (1, 0), (2, 1), (3, 1), (4, 0), (5, 1)):
                    self.sent(half[part], square + kind * net.line + z)
        if self.line:
            for z in range(net.line):
                pl.when((z <= net.z) & (net.z < net.line - 1))(lambda z=z: self.sent(own, right + z))
                pl.when((z >= net.z) & (net.z > 0))(lambda z=z: self.sent(own, left + z))


class Job:
    def __init__(self, arrays, outs, scratch, steps, where=pl.ANY, out_where=pl.ANY):
        self.arrays, self.outs, self.scratch, self.steps = arrays, outs, scratch, steps
        self.where, self.out_where = where, out_where


def together_kernel(line, jobs, order, *refs):
    refs = list(refs)
    take = lambda count: [refs.pop(0) for _ in range(count)]
    ins = [take(len(job.arrays)) for job in jobs]
    outs = [take(len(job.outs)) for job in jobs]
    scratch = [take(len(job.scratch)) for job in jobs]
    net = Net(line)
    net.greet([net.x, net.y, net.core] + net.others())
    chains, ends = [], []
    for job, *parts in zip(jobs, ins, outs, scratch):
        more, last = job.steps(net, *parts)
        chains += more
        ends += last
    for turn in order:
        next(chains[turn], None)
    while chains:
        chains = [chain for chain in chains if next(chain, True) is None]
    for end in ends:
        end()


def together(collective_id, name, sizes, jobs):
    line = sizes["mem"] // 2
    moved = sum(2 * a.size * a.dtype.itemsize for job in jobs for a in job.arrays)
    results = pl.pallas_call(
        functools.partial(together_kernel, line, jobs, ORDERS.get((name, line), ())),
        out_shape=[out for job in jobs for out in job.outs],
        in_specs=[pl.BlockSpec(memory_space=job.where) for job in jobs for _ in job.arrays],
        out_specs=[pl.BlockSpec(memory_space=job.out_where) for job in jobs for _ in job.outs],
        scratch_shapes=[s for job in jobs for s in job.scratch],
        compiler_params=params(collective_id=collective_id, has_side_effects=True),
        cost_estimate=pl.CostEstimate(flops=0, bytes_accessed=moved, transcendentals=0),
        name=name,
    )(*[a for job in jobs for a in job.arrays])
    results = list(results)
    return [[results.pop(0) for _ in job.outs] for job in jobs]


def gather_job(sizes, array, halves, reach, pieces=1):
    line = sizes["mem"] // 2
    slots = {"all": sizes["seq"] * sizes["mem"], "line": sizes["mem"], "square": sizes["seq"]}[reach]
    index = {
        "all": lambda s, z, c: (s * line + z) * 2 + c,
        "line": lambda s, z, c: z * 2 + c,
        "square": lambda s, z, c: s,
    }[reach]
    rows = array.shape[0] // pieces

    def steps(net, ins, outs, scratch):
        parts = []
        for i in range(pieces):
            span = pl.ds(i * rows, rows)
            src, out = (ins[0], outs[0]) if pieces == 1 else (ins[0].at[span], outs[0].at[:, span])
            parts.append(
                Gather(
                    net, src, out, *scratch[3 * i : 3 * i + 3], index, halves,
                    line=reach != "square", square=reach != "line", core=reach != "square",
                )
            )
        return [chain for part in parts for chain in part.chains()], [part.finish for part in parts]

    semaphores = [pltpu.SemaphoreType.DMA((15 * line,))] * 2 + [pltpu.SemaphoreType.DMA]
    out = jax.ShapeDtypeStruct((slots,) + array.shape, array.dtype)
    return Job([array], [out], semaphores * pieces, steps)


class Scatter:
    def __init__(self, net, src, out, buffers, sems, halves, whole=True):
        self.net, self.src, self.out, self.halves = net, src, out, halves
        self.whole, self.count = whole, src.shape[1]
        self.held, self.twin, self.first, self.second, self.along = buffers
        self.sends, self.recvs, self.own = sems

    def send(self, block, target, place, device):
        remote(block, target, self.sends, self.recvs, place, device).start()

    def sent(self, block, place):
        remote(block, block, self.sends, self.recvs, place, self.net.core).wait_send()

    def arrived(self, block, place):
        remote(block, block, self.sends, self.recvs, place, self.net.core).wait_recv()

    def places(self):
        z = self.count
        return 0, 4 * z, 8 * z, 10 * z, 11 * z

    def loading(self, d):
        source = self.src.at[:, d, self.net.c] if self.whole else self.src.at[:, d]
        return pltpu.make_async_copy(source, self.held.at[:, d], self.own.at[d])

    def load(self, d):
        net = self.net
        self.loading(d).start()
        for s in range(4 if self.whole else 0):
            self.send(self.src.at[s, d, 1 - net.c], self.twin.at[s, d], s * self.count + d, net.core)

    def add_core(self, d):
        net = self.net
        _, first, _, _, _ = self.places()
        self.loading(d).wait()
        for turn in (3, 2, 1, 0):
            s = net.s ^ turn
            if self.whole:
                self.arrived(self.twin.at[s, d], s * self.count + d)
                self.held[s, d] = self.held[s, d] + self.twin[s, d]
            for part, device, slot, kind in {
                3: ((0, net.y, 1, 1), (1, net.x, 1, 3)),
                2: ((0, net.y, 0, 0),),
                1: ((1, net.x, 0, 2),),
                0: (),
            }[turn]:
                self.send(
                    self.halves(self.held.at[s, d], part),
                    self.first.at[part, slot, d],
                    first + kind * self.count + d,
                    device,
                )

    def chain(self, k):
        d = lax.rem(self.net.z + k, self.net.line) if self.whole else k
        for stage in (self.load, self.add_core, self.add_first, self.add_second, self.line_step):
            stage(d)
            yield

    def add(self, block, other):
        block[...] = block[...] + other[...]

    def add_first(self, d):
        net = self.net
        _, first, second, _, _ = self.places()
        for part, slot, kind, turn in ((0, 1, 1, 1), (1, 1, 3, 2), (0, 0, 0, 0), (1, 0, 2, 0)):
            got = self.first.at[part, slot, d]
            self.arrived(got, first + kind * self.count + d)
            block = self.halves(self.held.at[net.s ^ turn, d], part)
            self.add(block, got)
            if turn:
                device = net.x if part == 0 else net.y
                self.send(block, self.second.at[part, d], second + part * self.count + d, device)

    def add_second(self, d):
        net = self.net
        _, _, second, _, _ = self.places()
        for part in range(2):
            self.arrived(self.second.at[part, d], second + part * self.count + d)
            self.add(self.halves(self.held.at[net.s, d], part), self.second.at[part, d])

    def line_step(self, d):
        net = self.net
        _, _, _, right, left = self.places()
        block = self.held.at[net.s, d]
        if not self.whole:
            self.out[d] = block[...].astype(self.out.dtype)
            return

        def go():
            pltpu.make_async_remote_copy(
                src_ref=block,
                dst_ref=self.along.at[net.z],
                send_sem=self.sends.at[right + d],
                recv_sem=self.recvs.at[left + net.z],
                device_id=(net.s, 2 * d + net.c),
                device_id_type=MESH,
            ).start()

        pl.when(net.z != d)(go)

    def keep(self):
        net = self.net
        _, _, _, _, left = self.places()
        total = self.held[net.s, net.z].astype(F32)
        for k in range(1, net.line):
            z = lax.rem(net.z + k, net.line)
            self.arrived(self.along.at[z], left + z)
            total = total + self.along[z].astype(F32)
        self.out[...] = total

    def finish(self):
        net = self.net
        _, first, second, right, left = self.places()
        full = self.held.at[net.s, 0]
        if self.whole:
            self.keep()
        for d in range(self.count):
            for s in range(4 if self.whole else 0):
                self.sent(full, s * self.count + d)
            for kind, part in enumerate((0, 0, 1, 1)):
                self.sent(self.halves(full, part), first + kind * self.count + d)
            for part in range(2):
                self.sent(self.halves(full, part), second + part * self.count + d)
            if self.whole:
                pl.when(net.z != d)(lambda d=d: self.sent(full, right + d))


def far_first(count):
    return sorted(range(count), key=lambda k: (k == 0, -min(k, count - k)))


def scatter_job(sizes, array, halves, whole=True):
    square, line = sizes["seq"], sizes["mem"] // 2
    columns = array.shape[1]
    if whole:
        count, rows = line, array.shape[0] // (2 * square * line)
        array = array.reshape(square, line, 2, rows, columns)
        out = jax.ShapeDtypeStruct((rows, columns), F32)
    else:
        count, rows = PIECES, array.shape[0] // (square * PIECES)
        array = array.reshape(square, count, rows, columns)
        out = jax.ShapeDtypeStruct((count, rows, columns), F32)
    half = (rows // 2, columns) if halves is row_halves else (rows, columns // 2)
    block, unused = (rows, columns), (16, 128)
    scratch = [
        pltpu.VMEM((4, count) + block, BF16),
        pltpu.VMEM((4, count) + block if whole else unused, BF16),
        pltpu.VMEM((2, 2, count) + half, BF16),
        pltpu.VMEM((2, count) + half, BF16),
        pltpu.VMEM((count,) + block if whole else unused, BF16),
        pltpu.SemaphoreType.DMA((12 * count,)),
        pltpu.SemaphoreType.DMA((12 * count,)),
        pltpu.SemaphoreType.DMA((count,)),
    ]

    def steps(net, ins, outs, scratch):
        scatter = Scatter(net, ins[0], outs[0], scratch[:5], scratch[5:], halves, whole)
        return [scatter.chain(k) for k in far_first(count)], [scatter.finish]

    return Job([array], [out], scratch, steps, out_where=pltpu.VMEM)


class Return:
    def __init__(self, net, sources, outs, scratch):
        kinds = len(sources)
        self.net, self.sources, self.outs, self.kinds = net, sources, outs, range(kinds)
        self.held, self.twin = scratch[:kinds], scratch[kinds : 2 * kinds]
        self.own, self.twin_sends, self.twin_recvs, self.sends, self.recvs = scratch[2 * kinds :]

    def loading(self, i, d):
        source = self.sources[i].at[d, self.net.c]
        return pltpu.make_async_copy(source, self.held[i].at[d], self.own.at[i, d])

    def pairing(self, i, d):
        net = self.net
        return remote(
            self.sources[i].at[d, 1 - net.c],
            self.twin[i].at[d],
            self.twin_sends.at[i],
            self.twin_recvs.at[i],
            d,
            net.core,
        )

    def giving(self, i, k, d, slot, device):
        return pltpu.make_async_remote_copy(
            src_ref=self.held[i].at[d],
            dst_ref=self.outs[i].at[slot],
            send_sem=self.sends.at[i, k],
            recv_sem=self.recvs.at[i, slot],
            device_id=device,
            device_id_type=MESH,
        )

    def keeping(self, i, d):
        return pltpu.make_async_copy(
            self.held[i].at[d], self.outs[i].at[self.net.z], self.own.at[i, d]
        )

    def chain(self, k):
        net = self.net
        d = lax.rem(net.z + k, net.line)
        for i in self.kinds:
            self.loading(i, d).start()
            self.pairing(i, d).start()
        yield
        for i in self.kinds:
            self.loading(i, d).wait()
            self.pairing(i, d).wait_recv()
        self.merge(d)
        for i in self.kinds:
            if k:
                self.giving(i, k, d, net.z, (net.s, 2 * d + net.c)).start()
            else:
                self.keeping(i, d).start()
        yield

    def merge(self, d):
        held, twin = self.held, self.twin
        if len(held) == 1:
            held[0][d] = held[0][d] + twin[0][d]
            return
        mine, theirs = held[1][d], twin[1][d]
        top = jnp.maximum(mine[:HEADS], theirs[:HEADS])
        shares = [jnp.exp2(mine[:HEADS] - top), jnp.exp2(theirs[:HEADS] - top)]
        held[1][d] = jnp.concatenate(
            [top, mine[HEADS:] * shares[0] + theirs[HEADS:] * shares[1]], axis=0
        )
        shares = columns_of(jnp.concatenate(shares, axis=0))
        for h in range(HEADS):
            span = slice(h * 128, (h + 1) * 128)
            held[0][d, :, span] = (
                held[0][d, :, span].astype(F32) * shares[:, h : h + 1]
                + twin[0][d, :, span].astype(F32) * shares[:, HEADS + h : HEADS + h + 1]
            ).astype(BF16)

    def finish(self):
        net = self.net
        for k in range(net.line):
            d = lax.rem(net.z + k, net.line)
            for i in self.kinds:
                self.pairing(i, d).wait_send()
                if k:
                    copy = self.giving(i, k, d, d, net.core)
                    copy.wait_recv()
                    copy.wait_send()
                else:
                    self.keeping(i, d).wait()


def return_job(sizes, arrays):
    line, kinds = sizes["mem"] // 2, len(arrays)
    blocks = [a.reshape((line, 2) + a.shape[1:]) for a in arrays]
    slots = [pltpu.VMEM((line,) + a.shape[1:], a.dtype) for a in arrays]
    outs = [jax.ShapeDtypeStruct((line,) + a.shape[1:], a.dtype) for a in arrays]
    scratch = slots + slots + [pltpu.SemaphoreType.DMA((kinds, line))] * 5
    def steps(net, ins, outs, scratch):
        back = Return(net, ins, outs, scratch)
        return [back.chain(k) for k in (*range(1, line), 0)], [back.finish]

    return Job(blocks, outs, scratch, steps)


def mask_words(index, base, mem_dev, place_ref, bit_ref):
    relative = index - base
    inside = (relative >= 0) & (relative < mem_dev)
    place = jnp.where(inside, relative & 127, 0)
    bit = jnp.where(inside, lax.shift_left(jnp.ones_like(relative), relative >> 7), 0)
    place_ref[...] = place.T
    bit_ref[...] = bit.T
    sought = lax.broadcasted_iota(jnp.int32, (128, 128), 0)
    halves = []
    for start in range(0, index.shape[0], 128):

        def eight(g, words, start=start):
            group = pl.ds(pl.multiple_of(g * 8, 8), 8)
            places = place_ref[group, start : start + 128]
            bits = bit_ref[group, start : start + 128]
            for j in range(8):
                words = words | jnp.where(places[j : j + 1] == sought, bits[j : j + 1], 0)
            return words

        none = jnp.zeros((128, 128), jnp.int32)
        words = lax.fori_loop(0, index.shape[1] // 8, eight, none)
        halves.append(words.T)
    return jnp.concatenate(halves, axis=0)


def mask_scratch(rows, count):
    return [pltpu.VMEM((count, rows), jnp.int32), pltpu.VMEM((count, rows), jnp.int32)]


def mask_kernel(mem_dev, base_ref, index_ref, bits_ref, place_ref, bit_ref):
    bits_ref[0] = mask_words(index_ref[0], base_ref[0], mem_dev, place_ref, bit_ref)


def mask_bits(base, all_index, mem_dev):
    segments, rows, count = all_index.shape
    return pl.pallas_call(
        functools.partial(mask_kernel, mem_dev),
        grid_spec=pltpu.PrefetchScalarGridSpec(
            num_scalar_prefetch=1,
            grid=(segments,),
            in_specs=[pl.BlockSpec((1, rows, count), lambda g, b: (g, 0, 0))],
            out_specs=pl.BlockSpec((1, rows, 128), lambda g, b: (g, 0, 0)),
            scratch_shapes=mask_scratch(rows, count),
        ),
        out_shape=jax.ShapeDtypeStruct((segments, rows, 128), jnp.int32),
        compiler_params=params(),
        name="mask_bits",
    )(base, all_index)


def mask_job(all_index, mem_dev):
    segments, rows, count = all_index.shape

    def steps(net, ins, outs, scratch):
        def chain():
            for g in range(segments):
                outs[0][g] = mask_words(ins[0][g], net.m * mem_dev, mem_dev, *scratch)
                yield

        return [chain()], []

    out = jax.ShapeDtypeStruct((segments, rows, 128), jnp.int32)
    return Job([all_index], [out], mask_scratch(rows, count), steps, pltpu.VMEM, pltpu.VMEM)


def fill_bias(bits_ref, bias_ref):
    bits = bits_ref[0]
    for b in range(bias_ref.shape[1] // 128):
        bias_ref[:, b * 128 : (b + 1) * 128] = jnp.where(((bits >> b) & 1) != 0, 0.0, FLOOR)


def owner_forward_kernel(scale, order_ref, q_ref, bits_ref, k_ref, v_ref, o_ref, st_ref, bias_ref):
    del order_ref
    fill_bias(bits_ref, bias_ref)
    maxima, sums = [], []
    for h in range(HEADS):
        span = slice(h * 128, (h + 1) * 128)
        scores = dot(q_ref[0, :, span], k_ref[0, :, span], NT) * scale + bias_ref[...]
        top = jnp.maximum(jnp.max(scores, axis=1, keepdims=True), LOW)
        weights = jnp.exp2(scores - top)
        maxima.append(top)
        sums.append(jnp.sum(weights, axis=1, keepdims=True))
        o_ref[0, :, span] = dot(weights.astype(BF16), v_ref[0, :, span]).astype(BF16)
    st_ref[0] = spread(maxima + sums).T[:STATS]


def owner_forward(order, queries, bits, cached_keys, cached_values, scale):
    segments, rows, width = queries.shape
    mem_dev = cached_keys.shape[1]
    active = order.shape[0]
    picked = lambda a, o: (o[a], 0, 0)
    return pl.pallas_call(
        functools.partial(owner_forward_kernel, scale),
        grid_spec=pltpu.PrefetchScalarGridSpec(
            num_scalar_prefetch=1,
            grid=(active,),
            in_specs=[
                pl.BlockSpec((1, rows, width), picked),
                pl.BlockSpec((1, rows, 128), picked),
                pl.BlockSpec((1, mem_dev, width), picked),
                pl.BlockSpec((1, mem_dev, width), picked),
            ],
            out_specs=[
                pl.BlockSpec((1, rows, width), picked),
                pl.BlockSpec((1, STATS, rows), picked),
            ],
            scratch_shapes=[pltpu.VMEM((rows, mem_dev), F32)],
        ),
        out_shape=[
            jax.ShapeDtypeStruct((segments, rows, width), BF16),
            jax.ShapeDtypeStruct((segments, STATS, rows), F32),
        ],
        compiler_params=params(),
        name="owner_forward",
    )(order, queries, bits, cached_keys, cached_values)


def owner_backward_kernel(
    scale, order_ref, q_ref, g_ref, st_ref, bits_ref, k_ref, v_ref, dq_ref, bias_ref
):
    del order_ref
    fill_bias(bits_ref, bias_ref)
    stats = columns_of(st_ref[0])
    for h in range(HEADS):
        span = slice(h * 128, (h + 1) * 128)
        scores = dot(q_ref[0, :, span], k_ref[0, :, span], NT) * scale + bias_ref[...]
        weights = jnp.exp2(scores - stats[:, h : h + 1])
        dweights = dot(g_ref[0, :, span], v_ref[0, :, span], NT)
        dscore = weights * (dweights - stats[:, HEADS + h : HEADS + h + 1])
        dq_ref[0, :, span] = (
            dot(dscore.astype(BF16), k_ref[0, :, span]) * (scale / LOG2E)
        ).astype(BF16)


def owner_backward(order, queries, grads, stats, bits, cached_keys, cached_values, scale):
    segments, rows, width = queries.shape
    mem_dev = cached_keys.shape[1]
    active = order.shape[0]
    picked = lambda a, o: (o[a], 0, 0)
    return pl.pallas_call(
        functools.partial(owner_backward_kernel, scale),
        grid_spec=pltpu.PrefetchScalarGridSpec(
            num_scalar_prefetch=1,
            grid=(active,),
            in_specs=[
                pl.BlockSpec((1, rows, width), picked),
                pl.BlockSpec((1, rows, width), picked),
                pl.BlockSpec((1, STATS, rows), picked),
                pl.BlockSpec((1, rows, 128), picked),
                pl.BlockSpec((1, mem_dev, width), picked),
                pl.BlockSpec((1, mem_dev, width), picked),
            ],
            out_specs=pl.BlockSpec((1, rows, width), picked),
            scratch_shapes=[pltpu.VMEM((rows, mem_dev), F32)],
        ),
        out_shape=jax.ShapeDtypeStruct((segments, rows, width), BF16),
        compiler_params=params(),
        name="owner_backward",
    )(order, queries, grads, stats, bits, cached_keys, cached_values)


def causal_bias(place, rows, keys):
    row = place * rows + lax.broadcasted_iota(jnp.int32, (rows, keys), 0)
    return jnp.where(lax.broadcasted_iota(jnp.int32, (rows, keys), 1) <= row, 0.0, FLOOR)


def local_forward_steps(scale, place, q_ref, kv_ref, o_ref, st_ref, bias_ref):
    rows, width = q_ref.shape
    bias_ref[...] = causal_bias(place, rows, kv_ref.shape[0])
    maxima, sums = [], []
    for h in range(HEADS):
        span, over = slice(h * 128, (h + 1) * 128), slice(width + h * 128, width + (h + 1) * 128)
        scores = dot(q_ref[:, span], kv_ref[:, span], NT) * scale + bias_ref[...]
        top = jnp.max(scores, axis=1, keepdims=True)
        weights = jnp.exp2(scores - top)
        maxima.append(top)
        sums.append(jnp.sum(weights, axis=1, keepdims=True))
        o_ref[:, span] = dot(weights.astype(BF16), kv_ref[:, over])
        yield
    st_ref[...] = spread(maxima + sums).T[:STATS]


def local_backward_steps(
    scale, place, q_ref, g_ref, st_ref, kv_ref, dq_ref, dkv_ref, bias_ref
):
    rows, width = q_ref.shape
    bias_ref[...] = causal_bias(place, rows, kv_ref.shape[0])
    stats = columns_of(st_ref[...])
    for h in range(HEADS):
        span, over = slice(h * 128, (h + 1) * 128), slice(width + h * 128, width + (h + 1) * 128)
        query, key, grad = q_ref[:, span], kv_ref[:, span], g_ref[:, span]
        scores = dot(query, key, NT) * scale + bias_ref[...]
        weights = jnp.exp2(scores - stats[:, h : h + 1])
        dweights = dot(grad, kv_ref[:, over], NT)
        dscore = (weights * (dweights - stats[:, HEADS + h : HEADS + h + 1])).astype(BF16)
        dq_ref[:, span] = dot(dscore, key) * (scale / LOG2E)
        dkv_ref[:, span] = (dot(dscore, query, TN) * (scale / LOG2E)).astype(BF16)
        dkv_ref[:, over] = dot(weights.astype(BF16), grad, TN).astype(BF16)
        yield


def local_job(kind, arrays, scale):
    rows, width = arrays[0].shape
    length = arrays[-1].shape[0]
    if kind == "forward":
        body, extra = local_forward_steps, jax.ShapeDtypeStruct((STATS, rows), F32)
    else:
        body, extra = local_backward_steps, jax.ShapeDtypeStruct((length, 2 * width), BF16)

    def steps(net, ins, outs, scratch):
        return [body(scale, net.s, *ins, *outs, *scratch)], []

    outs = [jax.ShapeDtypeStruct((rows, width), F32), extra]
    return Job(arrays, outs, [pltpu.VMEM((rows, length), F32)], steps, pltpu.VMEM, pltpu.VMEM)


def alone_kernel(job, *refs):
    place_ref, *refs = refs
    net = type("Alone", (), {"s": place_ref[0]})
    ins, outs = len(job.arrays), len(job.arrays) + len(job.outs)
    for chain in job.steps(net, refs[:ins], refs[ins:outs], refs[outs:])[0]:
        for _ in chain:
            pass


def alone(name, place, job):
    return pl.pallas_call(
        functools.partial(alone_kernel, job),
        out_shape=job.outs,
        in_specs=[pl.BlockSpec(memory_space=pltpu.SMEM)]
        + [pl.BlockSpec(memory_space=pltpu.VMEM)] * len(job.arrays),
        out_specs=[pl.BlockSpec(memory_space=pltpu.VMEM)] * len(job.outs),
        scratch_shapes=job.scratch,
        compiler_params=params(),
        name=name,
    )(place, *job.arrays)


def copy_in(pairs, sems):
    copies = [pltpu.make_async_copy(src, dst, sems.at[i]) for i, (src, dst) in enumerate(pairs)]
    for copy in copies:
        copy.start()
    return copies


def turn(values, cosine, sine):
    return values * cosine + pltpu.roll(values, values.shape[1] // 2, 1) * sine


def inverse_root(values):
    return lax.rsqrt(jnp.mean(values * values, axis=1, keepdims=True) + EPSILON)


def project_kernel(x_ref, w_any, cos_ref, sin_ref, n_ref, q_ref, kv_ref, gain_ref, w_ref, sems):
    width = x_ref.shape[1]
    spans = [slice(i * width, (i + 1) * width) for i in range(3)] + [slice(3 * width, 3 * width + 128)]
    copies = copy_in([(w_any.at[:, s], w_ref.at[:, s]) for s in spans], sems)
    x = x_ref[...].astype(F32)
    copies[3].wait()
    gain_ref[...] = w_ref[:, spans[3]].astype(F32).T[:8]
    normed = (x * inverse_root(x) * gain_ref[:1]).astype(BF16)
    n_ref[...] = normed
    cosine, sine = cos_ref[...], sin_ref[...]
    for i in range(3):
        copies[i].wait()
        product = dot(normed, w_ref[:, spans[i]])
        for h in range(HEADS):
            span = slice(h * 128, (h + 1) * 128)
            part = product[:, span]
            part = part if i == 2 else turn(part, cosine, sine)
            if i == 0:
                q_ref[:, span] = part.astype(BF16)
            else:
                over = slice((i - 1) * width + h * 128, (i - 1) * width + (h + 1) * 128)
                kv_ref[:, over] = part.astype(BF16)


def in_vmem(count):
    return [pl.BlockSpec(memory_space=pltpu.VMEM)] * count


def project(tokens, first_weights, cosine, sine):
    rows, width = tokens.shape
    columns = first_weights.shape[1]
    return pl.pallas_call(
        project_kernel,
        out_shape=[
            jax.ShapeDtypeStruct((rows, width), BF16),
            jax.ShapeDtypeStruct((rows, width), BF16),
            jax.ShapeDtypeStruct((rows, 2 * width), BF16),
            jax.ShapeDtypeStruct((8, width), F32),
        ],
        in_specs=in_vmem(1) + [pl.BlockSpec(memory_space=pl.ANY)] + in_vmem(2),
        out_specs=in_vmem(4),
        scratch_shapes=[
            pltpu.VMEM((width, columns), BF16),
            pltpu.SemaphoreType.DMA((4,)),
        ],
        compiler_params=params(),
        name="project",
    )(tokens, first_weights, cosine, sine)


def middle_kernel(
    live_ref, x_ref, g_ref, gain_ref, lo_ref, ls_ref, po_ref, ps_ref, out_any, gate_any, up_any, down_any,
    mixed_ref, gm_ref, al_ref, n_ref, gml_ref, ga_ref, st_ref, hid_ref, gg_ref, gu_ref, gain_grad_ref,
    att_ref, acc_ref, gn_ref, out_ref, gate_ref, up_ref, down_ref, sems,
):
    rows, width = x_ref.shape
    copies = copy_in(
        [(out_any, out_ref), (gate_any, gate_ref), (up_any, up_ref), (down_any, down_ref)], sems
    )
    live = live_ref[0] > 0
    peers = ps_ref.shape[0]
    local_max, local_sum = ls_ref[:HEADS], ls_ref[HEADS:]
    peer_max = [jnp.where(live, ps_ref[p, :HEADS], LOW) for p in range(peers)]
    peer_sum = [jnp.where(live, ps_ref[p, HEADS:], 0.0) for p in range(peers)]
    top = functools.reduce(jnp.maximum, peer_max, local_max)
    shares = [jnp.exp2(m - top) for m in [local_max] + peer_max]
    total = functools.reduce(
        jnp.add, [s * t for s, t in zip(shares, [local_sum] + peer_sum)]
    )
    log_total = top + jnp.log2(total)
    shares = columns_of(jnp.concatenate([s / total for s in shares], axis=0))
    for h in range(HEADS):
        span = slice(h * 128, (h + 1) * 128)
        part = lo_ref[:, span] * shares[:, h : h + 1]
        for p in range(peers):
            column = shares[:, (p + 1) * HEADS + h : (p + 1) * HEADS + h + 1]
            part += jnp.where(live, po_ref[p, :, span].astype(F32), 0.0) * column
        att_ref[:, span] = part
    attention_low = att_ref[...].astype(BF16)
    al_ref[...] = attention_low
    copies[0].wait()
    mid = x_ref[...].astype(F32) + dot(attention_low, out_ref[...])
    gm_ref[...] = mid
    root = inverse_root(mid)
    n_ref[...] = (mid * root * gain_ref[1:2]).astype(BF16)
    for copy in copies[1:]:
        copy.wait()
    grad = g_ref[...]
    acc_ref[...] = jnp.zeros_like(acc_ref)
    gn_ref[...] = jnp.zeros_like(gn_ref)
    hidden_width = gate_ref.shape[1]
    step = 256
    for start in range(0, hidden_width, step):
        span = slice(start, min(start + step, hidden_width))
        norm_two = n_ref[...]
        gate = dot(norm_two, gate_ref[:, span])
        upward = dot(norm_two, up_ref[:, span])
        grad_hidden = dot(grad, down_ref[span, :], NT)
        sigmoid = 1.0 / (1.0 + jnp.exp(-gate))
        silu = gate * sigmoid
        hidden = (silu * upward).astype(BF16)
        grad_gate = (grad_hidden * upward * (sigmoid * (1.0 + gate * (1.0 - sigmoid)))).astype(BF16)
        grad_up = (grad_hidden * silu).astype(BF16)
        hid_ref[:, span] = hidden
        gg_ref[:, span] = grad_gate
        gu_ref[:, span] = grad_up
        acc_ref[...] += dot(hidden, down_ref[span, :])
        gn_ref[...] += dot(grad_gate, gate_ref[:, span], NT) + dot(grad_up, up_ref[:, span], NT)
    mid = gm_ref[...]
    mixed_ref[...] = mid + acc_ref[...]
    normed = mid * root
    grad_norm = gn_ref[...]
    gain_grad_ref[...] = jnp.broadcast_to(
        jnp.sum(grad_norm * normed, axis=0, keepdims=True), gain_grad_ref.shape
    )
    scaled = grad_norm * gain_ref[1:2]
    grad_mid = grad.astype(F32) + root * (
        scaled - normed * jnp.mean(normed * scaled, axis=1, keepdims=True)
    )
    gm_ref[...] = grad_mid
    grad_mid_low = grad_mid.astype(BF16)
    gml_ref[...] = grad_mid_low
    grad_attention = dot(grad_mid_low, out_ref[...], NT).astype(BF16)
    ga_ref[...] = grad_attention
    products = grad_attention.astype(F32) * att_ref[...]
    dots = [
        jnp.sum(products[:, h * 128 : (h + 1) * 128], axis=1, keepdims=True) for h in range(HEADS)
    ]
    st_ref[...] = jnp.concatenate([log_total, spread(dots).T[:HEADS]], axis=0)


def middle(live, tokens, grads, gains, local, peers, weights):
    rows, width = tokens.shape
    hidden_width = weights[1].shape[1]
    full = lambda columns, kind: jax.ShapeDtypeStruct((rows, columns), kind)
    return pl.pallas_call(
        middle_kernel,
        out_shape=[
            full(width, F32),
            full(width, F32),
            full(width, BF16),
            full(width, BF16),
            full(width, BF16),
            full(width, BF16),
            jax.ShapeDtypeStruct((STATS, rows), F32),
            full(hidden_width, BF16),
            full(hidden_width, BF16),
            full(hidden_width, BF16),
            jax.ShapeDtypeStruct((8, width), F32),
        ],
        in_specs=[pl.BlockSpec(memory_space=pltpu.SMEM)]
        + in_vmem(7)
        + [pl.BlockSpec(memory_space=pl.ANY)] * 4,
        out_specs=in_vmem(11),
        scratch_shapes=[pltpu.VMEM((rows, width), F32)] * 3
        + [pltpu.VMEM(w.shape, BF16) for w in weights]
        + [pltpu.SemaphoreType.DMA((4,))],
        compiler_params=params(),
        name="middle",
    )(live, tokens, grads, gains, *local, *peers, *weights)


def final_kernel(
    live_ref, x_ref, gm_ref, gain_ref, ggain_ref, n_ref, dq_ref, pd_ref, dkv_ref, cos_ref, sin_ref, w_any,
    gx_ref, late_ref, in_ref, w_ref, sems,
):
    rows, width = x_ref.shape
    copies = copy_in([(w_any.at[:, : 3 * width], w_ref)], sems)
    live = live_ref[0] > 0
    cosine, sine = cos_ref[...], -sin_ref[...]
    for h in range(HEADS):
        span = slice(h * 128, (h + 1) * 128)
        part = dq_ref[:, span]
        for p in range(pd_ref.shape[0]):
            part += jnp.where(live, pd_ref[p, :, span].astype(F32), 0.0)
        in_ref[:, span] = turn(part, cosine, sine).astype(BF16)
        over = slice(width + h * 128, width + (h + 1) * 128)
        in_ref[:, over] = turn(dkv_ref[:, span], cosine, sine).astype(BF16)
    in_ref[:, 2 * width :] = dkv_ref[:, width:].astype(BF16)
    normed_low = n_ref[...]
    for i in range(3):
        span = slice(i * width, (i + 1) * width)
        late_ref[:, span] = dot(normed_low, in_ref[:, span], TN).astype(BF16)
    copies[0].wait()
    grad_norm = dot(in_ref[...], w_ref[...], NT)
    x = x_ref[...].astype(F32)
    root = inverse_root(x)
    normed = x * root
    gains = jnp.concatenate(
        [
            jnp.sum(grad_norm * normed, axis=0, keepdims=True),
            ggain_ref[:1],
            jnp.zeros((126, width), F32),
        ],
        axis=0,
    )
    late_ref[:, 3 * width :] = gains.T.astype(BF16)
    scaled = grad_norm * gain_ref[:1]
    gx_ref[...] = gm_ref[...] + root * (
        scaled - normed * jnp.mean(normed * scaled, axis=1, keepdims=True)
    )


def final(live, *arrays):
    rows, width = arrays[0].shape
    columns = arrays[-1].shape[1]
    return pl.pallas_call(
        final_kernel,
        out_shape=[
            jax.ShapeDtypeStruct((rows, width), F32),
            jax.ShapeDtypeStruct((width, columns), BF16),
        ],
        in_specs=[pl.BlockSpec(memory_space=pltpu.SMEM)]
        + in_vmem(len(arrays) - 1)
        + [pl.BlockSpec(memory_space=pl.ANY)],
        out_specs=in_vmem(2),
        scratch_shapes=[
            pltpu.VMEM((rows, 3 * width), BF16),
            pltpu.VMEM((width, 3 * width), BF16),
            pltpu.SemaphoreType.DMA((1,)),
        ],
        compiler_params=params(),
        name="final",
    )(live, *arrays)


REACH = {"all": ("seq", "mem"), "line": "mem", "square": "seq"}


def gather_plain(array, reach):
    return lax.all_gather(array, REACH[reach], axis=0)


def scatter_plain(array, reach):
    return lax.psum_scatter(array, REACH[reach], scatter_dimension=0, tiled=True).astype(F32)


def return_plain(array):
    return lax.all_to_all(array, "mem", split_axis=0, concat_axis=0, tiled=True)


def join_peers(outs, stats):
    top = jnp.max(stats[:, :HEADS], axis=0)
    shares = jnp.exp2(stats[:, :HEADS] - top)
    total = jnp.sum(stats[:, HEADS:] * shares, axis=0)
    wide = jnp.repeat(jnp.swapaxes(shares, 1, 2), outs.shape[-1] // HEADS, axis=2)
    joined = jnp.sum(outs.astype(F32) * wide, axis=0).astype(BF16)
    return joined[None], jnp.concatenate([top, total], axis=0)[None]


def per_device(
    sizes,
    tokens,
    cached_keys,
    cached_values,
    knn_index,
    has_memory,
    w_query,
    w_key,
    w_value,
    w_out,
    gain_attn,
    w_gate,
    w_up,
    w_down,
    gain_ffn,
    cotangent,
):
    near = sizes["seq"] == 4 and sizes["mem"] % 2 == 0 and 4 <= sizes["mem"] <= 16
    inputs, grad_out = tokens[0], cotangent[0]
    rows, width = inputs.shape
    hidden_width = w_gate.shape[1]
    head_width = width // HEADS
    scale = head_width ** (-0.5) * LOG2E
    mem_dev = cached_keys.shape[1]
    place = lax.axis_index("seq").astype(jnp.int32)[None]
    base = (lax.axis_index("mem") * mem_dev).astype(jnp.int32)[None]

    gains = jnp.concatenate(
        [gain_attn[:, None], gain_ffn[:, None], jnp.zeros((w_query.shape[0], 126), BF16)], axis=1
    )
    first_shard = jnp.concatenate([w_query, w_key, w_value, gains], axis=1)
    flag_rows = jnp.broadcast_to(has_memory[:, None], (8, 128))
    index_shard = jnp.concatenate([knn_index[0], flag_rows], axis=0)
    if near:
        jobs = [
            gather_job(sizes, index_shard, row_halves, "line"),
            gather_job(sizes, first_shard, row_halves, "all"),
        ]
        (shared,), (first_weights,) = together(1, "first", sizes, jobs)
    else:
        first_weights, shared = gather_plain(first_shard, "all"), gather_plain(index_shard, "line")
    first_weights = first_weights.reshape(-1, first_shard.shape[1])
    all_index, flags = shared[:, :rows], shared[:, rows, 0]
    segments = flags.shape[0]
    order = jnp.argsort(jnp.where(flags > 0, 0, 1), stable=True)[: segments // 2].astype(jnp.int32)

    positions = lax.axis_index("seq") * rows + jnp.arange(rows)
    cosine, sine = angles_for(positions, head_width)
    cosine = jnp.concatenate([cosine, cosine], axis=1)
    sine = jnp.concatenate([-sine, sine], axis=1)
    norm_one, queries, keys_values, gain_rows = project(inputs, first_weights, cosine, sine)
    if near:
        jobs = [
            gather_job(sizes, queries, row_halves, "line", PIECES),
            gather_job(sizes, keys_values, row_halves, "square"),
            gather_job(sizes, w_out, row_halves, "all"),
            mask_job(all_index, mem_dev),
        ]
        (all_queries,), (segment_kv,), (out_weight,), (bits,) = together(2, "second", sizes, jobs)
    else:
        all_queries = gather_plain(queries, "line")
        segment_kv = gather_plain(keys_values, "square")
        out_weight = gather_plain(w_out, "all")
        bits = mask_bits(base, all_index, mem_dev)
    segment_kv = segment_kv.reshape(-1, 2 * width)

    owner_out, owner_stats = owner_forward(
        order, all_queries, bits, cached_keys, cached_values, scale
    )
    local_work = local_job("forward", [queries, segment_kv], scale)
    if near:
        jobs = [
            return_job(sizes, [owner_out, owner_stats]),
            gather_job(sizes, w_gate, row_halves, "all"),
            gather_job(sizes, w_up, row_halves, "all"),
            gather_job(sizes, w_down, column_halves, "all"),
            local_work,
        ]
        peers, (gate_weight,), (up_weight,), (down_weight,), local = together(
            3, "third", sizes, jobs
        )
    else:
        peers = join_peers(return_plain(owner_out), return_plain(owner_stats))
        gate_weight, up_weight = gather_plain(w_gate, "all"), gather_plain(w_up, "all")
        down_weight = gather_plain(w_down, "all")
        local = alone("local_forward", place, local_work)
    weights = [
        out_weight.reshape(width, width),
        gate_weight.reshape(width, hidden_width),
        up_weight.reshape(width, hidden_width),
        down_weight.reshape(hidden_width, width),
    ]
    (
        mixed,
        grad_mid,
        attention_low,
        norm_two,
        grad_mid_low,
        grad_attention,
        back_stats,
        hidden,
        grad_gate,
        grad_upward,
        gain_two_grad,
    ) = middle(has_memory, inputs, grad_out, gain_rows, local, peers, weights)
    local_work = local_job(
        "backward", [queries, grad_attention, back_stats, segment_kv], scale
    )
    if near:
        jobs = [
            gather_job(sizes, grad_attention, row_halves, "line", PIECES),
            gather_job(sizes, back_stats, row_halves, "line"),
            local_work,
        ]
        (all_grads,), (all_stats,), (local_dq, local_dkv) = together(4, "fourth", sizes, jobs)
    else:
        all_grads, all_stats = gather_plain(grad_attention, "line"), gather_plain(back_stats, "line")
        local_dq, local_dkv = alone("local_backward", place, local_work)
    owner_grads = owner_backward(
        order, all_queries, all_grads, all_stats, bits, cached_keys, cached_values, scale
    )

    early = [
        dot(attention_low, grad_mid_low, TN).astype(BF16),
        dot(norm_two, grad_gate, TN).astype(BF16),
        dot(norm_two, grad_upward, TN).astype(BF16),
        dot(hidden, grad_out, TN).astype(BF16),
    ]
    if near:
        jobs = [
            return_job(sizes, [owner_grads]),
            scatter_job(sizes, local_dkv, row_halves, False),
            *[scatter_job(sizes, grad, row_halves) for grad in early[:3]],
            scatter_job(sizes, early[3], column_halves),
        ]
        (peer_grads,), (grad_kv,), *early_sums = together(5, "fifth", sizes, jobs)
        grad_kv = grad_kv.reshape(rows, 2 * width)
        early_sums = [total for (total,) in early_sums]
    else:
        peer_grads = jnp.sum(return_plain(owner_grads).astype(F32), axis=0, keepdims=True)
        grad_kv = scatter_plain(local_dkv, "square")
        early_sums = [scatter_plain(grad, "all") for grad in early]
    grad_inputs, late = final(
        has_memory, inputs, grad_mid, gain_rows, gain_two_grad, norm_one, local_dq, peer_grads, grad_kv,
        cosine, sine, first_weights,
    )
    if near:
        ((late_sum,),) = together(6, "sixth", sizes, [scatter_job(sizes, late, row_halves)])
    else:
        late_sum = scatter_plain(late, "all")
    return (
        mixed[None],
        grad_inputs[None],
        late_sum[:, :width],
        late_sum[:, width : 2 * width],
        late_sum[:, 2 * width : 3 * width],
        early_sums[0],
        late_sum[:, 3 * width],
        early_sums[1],
        early_sums[2],
        early_sums[3],
        late_sum[:, 3 * width + 1],
    )


def solution(mesh):
    rows, owned, feature = P("mem", "seq", None), P(None, "mem", None), P(("seq", "mem"), None)
    gain = P(("seq", "mem"))
    return jax.shard_map(
        functools.partial(per_device, dict(mesh.shape)),
        mesh=mesh,
        in_specs=(
            (rows, owned, owned, rows, P("mem"))
            + (feature,) * 4
            + (gain,)
            + (feature,) * 3
            + (gain, rows)
        ),
        out_specs=(rows, rows) + (feature,) * 4 + (gain,) + (feature,) * 3 + (gain,),
        check_vma=False,
    )
```

time: 1080 us -> 533 us (0.49)
  waiting for transfers between devices: 757 us -> 0 us
  Pallas kernels: 101 us -> 494 us
  other arithmetic: 50.1 us -> 3.34 us
  matrix products: 53.8 us -> 15.9 us
  local copies, waits for them, and re-layouts: 41 us -> 13.2 us
  blocking collectives: 25.1 us -> 0 us
  starting transfers between devices: 21.8 us -> 0 us
  between operations: 15.4 us -> 1.71 us
    pallas_call x3 -> x9, Pallas kernels: 59.6 us -> 452 us  [the longest x6 411 us: together(): pl.pallas_call(functools.partial(together_kernel, line, jobs, ORDERS.get(...]
    reduce_scatter x5 -> x0, waiting for transfers between devices: 368 us -> none  [the longest x1 163 us: per_device(): early_sum = scatter(early, both)]
    all_gather x8 -> x0, waiting for transfers between devices: 275 us -> none  [the longest x1 73 us: per_device(): out_gate_up = gather(jnp.concatenate([w_out, w_gate, w_up], axis=1), both)]
    all_to_all x2 -> x0, waiting for transfers between devices: 113 us -> none  [the longest x1 113 us: per_device(): peer_grads = exchange(owner_grads)]
    dot_general x15 -> x4, matrix products: 53.8 us -> 15.9 us  [dot(): return lax.dot_general(left, right, dims, preferred_element_type=F32)]
    concatenate x7 -> x1, other arithmetic: 17.3 us -> 0.84 us  [per_device(): cosine = jnp.concatenate([cosine, cosine], axis=1)]
    all_gather x1 -> x0, blocking collectives: 15 us -> none  [per_device(): gather(back_stats[None], 'mem')]
    all_gather x8 -> x0, starting transfers between devices: 11.6 us -> none  [the longest x1 11.3 us: per_device(): gather(grad_attention[None], 'mem')]
  transfers between devices with their start and end apart: 15 -> 0, of which waited for: 11 -> 0; matrix products, arithmetic and copies ran while one was open for 11% -> 0% of each run, Pallas kernels for 9% -> 0%
where the time goes in v3:
time: 533 us; the launch traced here: 528 us
  Pallas kernels  494 us (93%)
  matrix products  15.9 us (3%)
  local copies, waits for them, and re-layouts  13.2 us (2%)
    pallas_call x6, Pallas kernels, together(): pl.pallas_call(functools.partial(together_kernel, line, jobs, ORDERS.get(...  411 us
    pallas_call x1, Pallas kernels, middle(): pl.pallas_call(middle_kernel, out_shape=[full(width, F32), full(width, F3...  21.8 us
    pallas_call x1, Pallas kernels, owner_backward(): pl.pallas_call(functools.partial(owner_backward_kernel, scale), grid_spec...  21.1 us
    pallas_call x1, Pallas kernels, owner_forward(): pl.pallas_call(functools.partial(owner_forward_kernel, scale), grid_spec=...  20.7 us
    dot_general x4, matrix products, dot(): return lax.dot_general(left, right, dims, preferred_element_type=F32)  15.9 us
    pallas_call x1, Pallas kernels, final(): pl.pallas_call(final_kernel, out_shape=[jax.ShapeDtypeStruct((rows, width...  11.3 us

profile of v3, /device:TPU:0, one launch (start us, length us, event | category | flops | bytes accessed | tf_op | source)
XLA Modules:
  0.0 527.7 jit_solution(7592325283997876506)
XLA Ops:
  1.3 0.8 copy.28
  2.1 0.8 copy.29
  2.8 1.6 concatenate.12.refs_0_
  4.4 1.7 concatenate.13.refs_1_
  6.1 0.5 fusion
  6.6 0.8 pad_maximum_fusion
  7.5 39.9 %first.1 = (s32[8,264,128]{2,1,0:T(8,128)}, bf16[32,32,3200]{2,1,0:T(8,128)(2,1)}) custom-call(s32[264,128]{1,0:T(8,128)} %concatenate.12.refs_0_, bf16[32,3200]{1,0:T(8,128)(2,1)} %concatenate.13.refs_1_), custom_call_target="tpu_custom_call" | custom-call | bytes 679936 | tf_op jit(solution)/shard_map/first/pallas_call | solution.py:289
  47.4 1.0 fusion.1
  48.3 2.3 slice.26.refs_3_
  50.6 1.0 sort.17
  51.6 7.7 %project.1 = (bf16[256,1024]{1,0:T(8,128)(2,1)}, bf16[256,1024]{1,0:T(8,128)(2,1)}, bf16[256,2048]{1,0:T(8,128)(2,1)}, f32[8,1024]{1,0:T(8,128)}) custom-call(bf16[256,1024]{1,0:T(8,128)(2,1)} %bitcast.48, bf16[1024,3200]{1,0:T(8,128)(2,1)} %bitcast.38, f32[256,128]{1,0:T(8,128)} %get-tuple-element.105.cos_ref, f32[256,128]{1,0:T(8,128)} %get-tuple-element.106.sin_ref), custom_call_target="tpu_custom_call" | custom-call | tf_op jit(solution)/shard_map/project/pallas_call | solution.py:878
  59.3 61.1 %second.1 = (bf16[8,256,1024]{2,1,0:T(8,128)(2,1)}, bf16[4,256,2048]{2,1,0:T(8,128)(2,1)}, bf16[32,32,1024]{2,1,0:T(8,128)(2,1)}, s32[8,256,128]{2,1,0:T(8,128)}) custom-call(bf16[256,1024]{1,0:T(8,128)(2,1)} %get-tuple-element.58.refs_0_.refs_5_.refs_2_, bf16[256,2048]{1,0:T(8,128)(2,1)} %get-tuple-element.59.refs_1_, bf16[32,1024]{1,0:T(8,128)(2,1)} %refs_2_.2, ...), custom_call_target="tpu_custom_call" | custom-call | bytes 5373952 | tf_op jit(solution)/shard_map/second/pallas_call | solution.py:289
  120.4 20.7 %owner_forward.1 = (bf16[8,256,1024]{2,1,0:T(8,128)(2,1)}, f32[8,16,256]{2,1,0:T(8,128)}) custom-call(s32[4]{0:T(128)} %bitcast.58, bf16[8,256,1024]{2,1,0:T(8,128)(2,1)} %get-tuple-element.60.q_ref, s32[8,256,128]{2,1,0:T(8,128)} %get-tuple-element.61.bits_ref, bf16[8,1024,1024]{2,1,0:T(8,128)(2,1)} %k_ref.3, bf16[8,1024,1024]{2,1,0:T(8,128)(2,1)} %v_ref.3), custom_call_target="tpu_custom_call" | custom-call | tf_op jit(solution)/shard_map/owner_forward/pallas_call | solution.py:685
  141.2 101.7 %third.1 = (bf16[4,256,1024]{2,1,0:T(8,128)(2,1)}, f32[4,16,256]{2,1,0:T(8,128)}, bf16[32,32,2816]{2,1,0:T(8,128)(2,1)}, bf16[32,32,2816]{2,1,0:T(8,128)(2,1)}, ...) custom-call(bf16[4,2,256,1024]{3,2,1,0:T(8,128)(2,1)} %bitcast.51, ...), custom_call_target="tpu_custom_call" | custom-call | bytes 19169280 | tf_op jit(solution)/shard_map/third/pallas_call | solution.py:289
  242.9 21.8 %middle.1 = (f32[256,1024]{1,0:T(8,128)}, f32[256,1024]{1,0:T(8,128)}, bf16[256,1024]{1,0:T(8,128)(2,1)}, bf16[256,1024]{1,0:T(8,128)(2,1)}, bf16[256,1024]{1,0:...) custom-call(s32[1]{0:T(128)} %copy.34.live_ref, ...), custom_call_target="tpu_custom_call" | custom-call | tf_op jit(solution)/shard_map/middle/pallas_call | solution.py:982
  264.7 3.3 convolution_convert_fusion.3
  268.1 48.0 %fourth.1 = (bf16[8,256,1024]{2,1,0:T(8,128)(2,1)}, f32[8,16,256]{2,1,0:T(8,128)}, f32[256,1024]{1,0:T(8,128)}, bf16[1024,2048]{1,0:T(8,128)(2,1)}) custom-call(bf16[256,1024]{1,0:T(8,128)(2,1)} %get-tuple-element.77.refs_0_.refs_3_, f32[16,256]{1,0:T(8,128)} %get-tuple-element.78.refs_1_.refs_4_, ...), custom_call_target="tpu_custom_call" | custom-call | bytes 11599872 | tf_op jit(solution)/shard_map/fourth/pallas_call | solution.py:289
  316.0 0.0 copy-start
  316.1 21.1 %owner_backward.1 = bf16[8,256,1024]{2,1,0:T(8,128)(2,1)} custom-call(s32[4]{0:T(128)} %bitcast.59, bf16[8,256,1024]{2,1,0:T(8,128)(2,1)} %get-tuple-element.60.q_ref, bf16[8,256,1024]{2,1,0:T(8,128)(2,1)} %get-tuple-element.80.g_ref, f32[8,16,256]{2,1,0:T(8,128)} %get-tuple-element.81.st_ref, s32[8,256,128]{2,1,0:T(8,128)} %get-tuple-element.61.bits_ref, ...), custom_call_target="tpu_custom_call" | custom-call | tf_op jit(solution)/shard_map/owner_backward/pallas_call | solution.py:733
  337.2 4.2 convolution_convert_fusion.2
  341.4 4.2 convolution_convert_fusion.1
  345.6 0.0 copy-done.1
  345.6 4.2 convolution_convert_fusion
  349.8 126.1 %fifth.1 = (bf16[4,256,1024]{2,1,0:T(8,128)(2,1)}, f32[4,64,2048]{2,1,0:T(8,128)}, f32[32,1024]{1,0:T(8,128)}, f32[32,2816]{1,0:T(8,128)}, f32[32,2816]{1,0:T(8,128)}, /*index=5*/f32[88,1024]{1,0:T(8,128)}) custom-call(bf16[4,2,256,1024]{3,2,1,0:T(8,128)(2,1)} %bitcast.42, bf16[4,4,64,2048]{3,2,1,0:T(8,128)(2,1)} %bitcast.52, ...), custom_call_target="tpu_custom_call" | custom-call | bytes 55574528 | tf_op jit(solution)/shard_map/fifth/pallas_call | solution.py:289
  475.9 11.3 %final.1 = (f32[256,1024]{1,0:T(8,128)}, bf16[1024,3200]{1,0:T(8,128)(2,1)}) custom-call(s32[1]{0:T(128)} %copy.34.live_ref, bf16[256,1024]{1,0:T(8,128)(2,1)} %bitcast.50, f32[256,1024]{1,0:T(8,128)} %get-tuple-element.74.gm_ref, f32[8,1024]{1,0:T(8,128)} %get-tuple-element.55.gain_ref, f32[8,1024]{1,0:T(8,128)} %get-tuple-element.75.ggain_ref, ...), custom_call_target="tpu_custom_call" | custom-call | tf_op jit(solution)/shard_map/final/pallas_call | solution.py:1053
  487.2 34.1 %sixth.1 = f32[32,3200]{1,0:T(8,128)} custom-call(bf16[4,4,2,32,3200]{4,3,2,1,0:T(8,128)(2,1)} %bitcast.44), custom_call_target="tpu_custom_call" | custom-call | bytes 13107200 | tf_op jit(solution)/shard_map/sixth/pallas_call | solution.py:289
  521.3 1.5 slice_reduce_fusion
  522.8 1.8 fusion.3
  524.6 0.7 copy.35
  525.3 0.7 copy.36
  526.0 0.7 copy.37
  526.7 0.7 copy.38
  (20 shorter events, 0.1 us)
Async XLA Ops:
  316.0 21.1 %copy-start = (bf16[256,1024]{1,0:T(8,128)(2,1)S(1)}, bf16[256,1024]{1,0:T(8,128)(2,1)}, u32[]{:S(2)}) copy-start(bf16[256,1024]{1,0:T(8,128)(2,1)} %get-tuple-element.85) | copy-start | bytes 1572868
  316.1 21.1 %copy-start.4 = (bf16[256,2816]{1,0:T(8,128)(2,1)S(1)}, bf16[256,2816]{1,0:T(8,128)(2,1)}, u32[]{:S(2)}) copy-start(bf16[256,2816]{1,0:T(8,128)(2,1)} %get-tuple-element.86) | copy-start | bytes 4325380
  337.2 4.2 copy-start.3
  341.4 4.2 copy-start.1
  341.4 4.2 copy-start.2
  487.2 37.5 %copy-start.8 = (f32[32,1024]{1,0:T(8,128)S(1)}, f32[32,1024]{1,0:T(8,128)}, u32[]{:S(2)}) copy-start(f32[32,1024]{1,0:T(8,128)} %get-tuple-element.123) | copy-start | bytes 393220
  487.2 38.1 %copy-start.7 = (f32[32,2816]{1,0:T(8,128)S(1)}, f32[32,2816]{1,0:T(8,128)}, u32[]{:S(2)}) copy-start(f32[32,2816]{1,0:T(8,128)} %get-tuple-element.125) | copy-start | bytes 1081348
  487.2 38.8 %copy-start.6 = (f32[32,2816]{1,0:T(8,128)S(1)}, f32[32,2816]{1,0:T(8,128)}, u32[]{:S(2)}) copy-start(f32[32,2816]{1,0:T(8,128)} %get-tuple-element.126) | copy-start | bytes 1081348
  487.2 39.6 %copy-start.5 = (f32[88,1024]{1,0:T(8,128)S(1)}, f32[88,1024]{1,0:T(8,128)}, u32[]{:S(2)}) copy-start(f32[88,1024]{1,0:T(8,128)} %get-tuple-element.127) | copy-start | bytes 1081348
